TPU v7x, 256 devices: a whole 4x4x8 slice. The times are simulated.
256 devices in a mesh: arc: 32 (over x_lo, z, core), col: 8 (over y, x_hi).
Axes of the slice: x: 4 (x_hi: 2, x_lo: 2; x = x_hi * 2 + x_lo), y: 4, z: 8, core: 2. Of those that a mesh axis runs over, the one named last changes fastest.
Arguments:
- force: float32 [3, 2048, 15360], P(None, 'arc', 'col'), may hold values from -0.8 to 0.8
- propagate: float32 [6, 6, 2048], P(None, None, 'arc'), may hold values from -0.02 to 1
- sight: float32 [6, 2048], P(None, 'arc'), may hold values from -2.4 to 2.4
- weights: float32 [2048], P('arc'), may hold values from 0.2 to 2
- lengths: int32 [32], replicated, may hold values from 1 to 192, 2048 in all
- order: int32 [32], replicated, may hold values from 0 to 31, each once
Outputs:
- normal: float32 [15360, 15360], P('arc', 'col')
Inputs may be any that keep to these rules, and one draw needn't show every extreme that they name: The lengths sum to 2048. `order`: each block number once.
All inputs are finite; a program needn't handle non-finite values.
Results may differ from a plain program's by a relative error of at most 0.00014.
Values sent between devices are 32-bit elements; how exact they have to be, the bound alone decides.
No kernel may reach another device: no remote copies, remote signals or barrier semaphores. Data moves between devices by JAX's collectives and lax.ppermute only.
A program may use at most 128 MiB of HBM per device.

v0:
```python
import jax
import jax.numpy as jnp
from jax import lax
from jax.sharding import PartitionSpec as P

HIGH = lax.Precision.HIGHEST


def prefix(value, axis, join, neutral):
    count, mine = (lax.axis_size(axis), lax.axis_index(axis))
    pieces = jax.tree.map(lambda part: lax.all_gather(part, axis), value)
    total = jax.tree.map(
        lambda part, zero: jnp.full_like(part, 0) + jnp.asarray(zero, part.dtype), value, neutral
    )

    def step(position, total):
        longer = join(total, jax.tree.map(lambda part: part[position], pieces))
        return jax.tree.map(lambda new, old: jnp.where(position < mine, new, old), longer, total)

    return lax.fori_loop(0, count - 1, step, total)


def chain_maps(earlier, later):
    matrix = jnp.einsum("tij,tjk->tik", later[0], earlier[0], precision=HIGH)
    offset = jnp.einsum("tij,tjk->tik", later[0], earlier[1], precision=HIGH) + later[1]
    return (matrix, offset)


def join_states(earlier, later):
    matrix = jnp.dot(later[0], earlier[0], precision=HIGH)
    offset = jnp.dot(later[0], earlier[1], precision=HIGH) + later[1]
    return (matrix, offset)


def contract_rows(left, right):
    return lax.dot_general(
        left, right, (((0,), (0,)), ((), ())), precision=HIGH, preferred_element_type=jnp.float32
    )


def body(force, propagate, sight, weights, lengths, order):
    epoch_dev = force.shape[1]
    width_col = force.shape[2]
    arc_count = lax.axis_size("arc")
    col_count = lax.axis_size("col")
    width_blk = width_col * col_count // arc_count
    every_epoch = epoch_dev * arc_count
    rank = lax.axis_index("arc")
    positions = rank * epoch_dev + jnp.arange(epoch_dev, dtype=jnp.int32)
    starts = jnp.cumsum(lengths) - lengths
    fresh = jnp.any(positions[:, None] == starts[None, :], axis=1)
    keep = jnp.where(fresh, 0.0, 1.0).astype(jnp.float32)
    transfer = jnp.moveaxis(propagate, 2, 0) * keep[:, None, None]
    inject = jnp.concatenate(
        [0.5 * jnp.eye(3, dtype=jnp.float32), jnp.eye(3, dtype=jnp.float32)], 0
    )
    picker = (jnp.arange(epoch_dev)[:, None] == jnp.arange(epoch_dev)[None, :]).astype(jnp.float32)
    kicks = (inject[None, :, :, None] * picker[:, None, None, :]).reshape(
        epoch_dev, 6, 3 * epoch_dev
    )
    cumul, reach = lax.associative_scan(chain_maps, (transfer, kicks))
    looking = jnp.transpose(sight)
    coeffs = jnp.einsum("ti,tik->tk", looking, reach, precision=HIGH)
    entry = jnp.einsum("ti,tij->tj", looking, cumul, precision=HIGH)
    flat_force = force.reshape(3 * epoch_dev, width_col)
    end_state = jnp.dot(reach[-1], flat_force, precision=HIGH)
    identity = (jnp.eye(6, dtype=jnp.float32), jnp.zeros((6, width_col), jnp.float32))
    _, incoming = prefix((cumul[-1], end_state), "arc", join_states, identity)
    design = jnp.dot(coeffs, flat_force, precision=HIGH) + jnp.dot(entry, incoming, precision=HIGH)
    scale = weights / every_epoch
    full = lax.all_gather(design, "col", axis=1, tiled=True)
    weighted = full * scale[:, None]
    grouped = jnp.take(weighted.reshape(epoch_dev, arc_count, width_blk), order, axis=1)
    moved = lax.all_to_all(grouped, "arc", split_axis=1, concat_axis=0, tiled=True)
    left = moved.reshape(every_epoch, width_blk)
    return contract_rows(left, lax.all_gather(design, "arc", axis=0, tiled=True))


def solution(mesh):
    in_specs = (P(None, "arc", "col"), P(None, None, "arc"), P(None, "arc"), P("arc"), P(), P())
    out_specs = P("arc", "col")
    return jax.shard_map(body, mesh=mesh, in_specs=in_specs, out_specs=out_specs, check_vma=False)
```

profile of v0, /device:TPU:3, one launch (start us, length us, event | category | flops | bytes accessed | tf_op | source)
XLA Modules:
  0.0 418.9 jit_solution(14111519674950381280)
XLA Ops:
  16.4 1.5 convolution_bitcast_fusion
  22.6 37.1 %all_gather.15 = f32[32,6,6]{2,1,0:T(8,128)S(1)} all-gather(f32[1,6,6]{2,1,0:T(8,128)S(1)} %slice_add_fusion), channel_id=1, replica_groups=mesh['arc'=32,'col'=8] {'arc'}, dimensions={0}, use_global_device_ids=true | all-gather | bytes 4752 | tf_op jit(solution)/shard_map/all_gather | solution.py:11
  61.0 24.5 %all-gather.10.cloned.1.call-done = f32[32,6,1920]{2,1,0:T(8,128)} async-done(((f32[1,6,1920]{2,1,0:T(8,128)}), f32[32,6,1920]{2,1,0:T(8,128)}) %all-gather.10.cloned.1.call-update) | async-done | bytes 1474576 | tf_op jit(solution)/shard_map/all_gather | solution.py:11
  85.5 33.2 %while.14 = (s32[]{:T(128)}, f32[6,1920]{1,0:T(8,128)S(1)}, s32[]{:T(128)}, f32[32,6,6]{2,1,0:T(8,128)S(1)}, f32[32,6,1920]{2,1,0:T(8,128)}, /*index=5*/s32[]{:T(128)}, s32[]{:T(128)}) while((s32[]{:T(128)}, f32[6,1920]{1,0:T(8,128)S(1)}, s32[]{:T(128)}, f32[32,6,6]{2,1,0:T(8,128)S(1)}, f32[32,6,1920]{2,1,0:T(8,128)}, ...), condition=%wide.region_3.4_spmd.clone, body=%wide.region_2.3_spmd.clone.sunk | while | flops 875524 | bytes 329311 | solution.py:20
  86.5 1.0 fusion.109
  87.6 1.0 fusion.109
  89.8 1.0 fusion.109
  90.8 1.0 fusion.109
  93.0 1.0 fusion.109
  94.0 1.0 fusion.109
  96.2 1.0 fusion.109
  97.3 1.0 fusion.109
  99.4 1.0 fusion.109
  102.6 1.0 fusion.109
  105.8 1.0 fusion.109
  106.9 1.0 fusion.109
  109.1 1.0 fusion.109
  110.1 1.0 fusion.109
  112.3 1.0 fusion.109
  113.4 1.0 fusion.109
  115.5 1.0 fusion.109
  116.6 1.0 fusion.109
  119.2 1.8 convolution_add_fusion.1
  121.9 72.1 %all-gather.6.cloned.1.call-done = f32[64,15360]{1,0:T(8,128)} async-done(((f32[64,1920]{1,0:T(8,128)}), f32[64,15360]{1,0:T(8,128)}) %all-gather.6.cloned.1.call-update) | async-done | bytes 3932176 | tf_op jit(solution)/shard_map/all_gather | solution.py:71
  193.9 4.4 %broadcast_multiply_fusion = f32[64,15360]{1,0:T(8,128)} fusion(f32[64,15360]{1,0:T(8,128)} %all-gather.6.cloned.1.call-done, f32[64]{0:T(128)S(1)} %broadcast_multiply_fusion.3), kind=kLoop, calls=%fused_computation.13 | loop fusion | flops 983040 | bytes 7864576 | tf_op jit(solution)/shard_map/mul | solution.py:72
  198.4 6.0 %reshape.100 = f32[64,32,480]{2,1,0:T(8,128)} reshape(f32[64,15360]{1,0:T(8,128)} %broadcast_multiply_fusion) | data formatting | bytes 7864320 | tf_op jit(solution)/shard_map/reshape | solution.py:73
  204.3 6.6 %copy.47 = f32[64,32,480]{2,0,1:T(8,128)} copy(f32[64,32,480]{2,1,0:T(8,128)} %reshape.100) | data formatting | bytes 7864320 | tf_op jit(solution)/shard_map/reshape | solution.py:73
  210.9 5.0 %gather_fusion = f32[32,64,480]{2,1,0:T(8,128)} fusion(f32[64,32,480]{2,0,1:T(8,128)} %copy.47, s32[1024]{0:T(1024)S(1)} %pad_clamp_fusion), kind=kCustom, calls=%fused_computation | custom fusion | bytes 7864448 | tf_op jit(solution)/shard_map/jit(_take)/gather | solution.py:73
  216.0 3.0 select_bitcast_fusion
  219.0 145.8 %all_to_all.15 = f32[64,32,480]{2,0,1:T(8,128)} all-to-all(f32[64,32,480]{2,0,1:T(8,128)S(1)} %select_bitcast_fusion), channel_id=1, replica_groups=mesh['arc'=32,'col'=8] {'arc'}, dimensions={1} | all-to-all | bytes 7864320 | tf_op jit(solution)/shard_map/all_to_all | solution.py:74
  364.8 15.0 %all-gather.8.cloned.1.call-done = f32[2048,1920]{1,0:T(8,128)} async-done(((f32[64,1920]{1,0:T(8,128)}), f32[2048,1920]{1,0:T(8,128)}) %all-gather.8.cloned.1.call-update) | async-done | bytes 15728656 | tf_op jit(solution)/shard_map/all_gather | solution.py:76
  379.7 32.6 %fusion.90 = f32[480,1920]{1,0:T(8,128)} fusion(f32[2048,480]{1,0:T(8,128)} %bitcast.85, f32[2048,1920]{1,0:T(8,128)} %all-gather.8.cloned.1.call-done), kind=kOutput, calls=%fused_computation.140 | convolution fusion | flops 22649241600 | bytes 23347200 | tf_op jit(solution)/shard_map/dot_general | solution.py:36
  (169 shorter events, 30.0 us)
Async XLA Ops:
  6.5 9.9 %copy-start = (f32[3,64,1920]{2,1,0:T(8,128)S(1)}, f32[3,64,1920]{2,1,0:T(8,128)}, u32[]{:S(2)}) copy-start(f32[3,64,1920]{2,1,0:T(8,128)} %param.8) | copy-start | bytes 4423684
  6.5 78.9 %all-gather.10.cloned.1.call-start = ((), (), s32[]{:S(2)}) async-start(), calls=%async_computation.3 | async-start | bytes 2027520 | tf_op jit(solution)/shard_map/all_gather | solution.py:11
  10.0 1.6 copy-start.2
  12.0 3.9 copy-start.1
  17.9 176.1 %all-gather.6.cloned.1.call-start = ((), (), s32[]{:S(2)}) async-start(), calls=%async_computation.1 | async-start | bytes 4423680 | tf_op jit(solution)/shard_map/all_gather | solution.py:71
  22.3 99.5 %copy-start.3 = (s32[32]{0:T(128)S(1)}, s32[32]{0:T(128)}, u32[]{:S(2)}) copy-start(s32[32]{0:T(128)} %param.13) | copy-start | bytes 388
  22.3 99.5 %copy-start.4 = (f32[64]{0:T(128)S(1)}, f32[64]{0:T(128)}, u32[]{:S(2)}) copy-start(f32[64]{0:T(128)} %param.11) | copy-start | bytes 772
  121.1 258.7 %all-gather.8.cloned.1.call-start = ((), (), s32[]{:S(2)}) async-start(), calls=%async_computation.2 | async-start | bytes 16220160 | tf_op jit(solution)/shard_map/all_gather | solution.py:76
Sparse Core Ops, SparseCore 0:
  18.0 67.4 all-gather.9
  121.2 72.7 all-gather.5
  195.8 183.9 all-gather.7
where the time goes:
time: 422 us; the launch traced here: 419 us
  blocking collectives  183 us (43%)
  waiting for transfers between devices  112 us (27%)
  matrix products  74.6 us (18%)
  local copies, waits for them, and re-layouts  23.8 us (6%)
  between operations  13.8 us (3%)
  other arithmetic  10.3 us (2%)
    all_to_all x1, blocking collectives, body(): lax.all_to_all(grouped, 'arc', split_axis=1, concat_axis=0, tiled=True)  146 us
    all_gather x1, waiting for transfers between devices, body(): full = lax.all_gather(design, 'col', axis=1, tiled=True)  72.1 us
    all_gather x1, blocking collectives, prefix(): pieces = jax.tree.map(lambda part: lax.all_gather(part, axis), value)  37.1 us
    dot_general x1, matrix products, contract_rows(): lax.dot_general(left, right, (((0,), (0,)), ((), ())), precision=HIGH, pr...  32.6 us
    dot_general x31, matrix products, join_states(): offset = jnp.dot(later[0], earlier[1], precision=HIGH) + later[1]  31.8 us
    all_gather x1, waiting for transfers between devices, prefix(): pieces = jax.tree.map(lambda part: lax.all_gather(part, axis), value)  24.5 us
    all_gather x1, waiting for transfers between devices, body(): lax.all_gather(design, 'arc', axis=0, tiled=True)  15 us
    reshape x2, local copies, waits for them, and re-layouts, body(): weighted.reshape(epoch_dev, arc_count, width_blk)  12.6 us
  transfers between devices with their start and end apart: 3, of which 3 were waited for; matrix products, arithmetic and copies ran while one was open for 7% of the time, Pallas kernels for 0%

commit v1 on v0

v1 whole, which is shorter than its diff:
```python
import functools

import jax
import jax.numpy as jnp
from jax import lax
from jax.experimental import pallas as pl
from jax.experimental.pallas import tpu as pltpu
from jax.sharding import PartitionSpec as P

HIGH = lax.Precision.HIGHEST
AXES = ("arc", "col")
XL, NZ, CO, NY, XH = 2, 8, 2, 4, 2
EPOCHS = 64
SLOTS = 8
WIDE = 1920
BLOCK = 480
EVERY = 2048
LAST = [(2, 0), (2, 1)]
EARLY = [(dy, dxh) for dy in (0, 1, 3) for dxh in range(XH)]
LATE = (NZ + 3, NZ + 4, NZ + 5, NZ + 6)
DEEP = 128 * len(LAST)
PICK = SLOTS * len(LATE) * len(EARLY)
MIB = 1 << 20
WHOLE = 60 * MIB
VMEM = pl.BlockSpec(memory_space=pltpu.VMEM)
SMEM = pl.BlockSpec(memory_space=pltpu.SMEM)
HBM = pl.BlockSpec(memory_space=pltpu.HBM)


def place(device):
    arc, col = divmod(device, NY * XH)
    xl, rest = divmod(arc, NZ * CO)
    z, core = divmod(rest, CO)
    y, xh = divmod(col, XH)
    return xl, z, core, y, xh


def number(xl, z, core, y, xh):
    return (((xl * NZ + z) * CO + core) * NY + y) * XH + xh


def send(value, dxl=0, dz=0, dcore=0, dy=0, dxh=0):
    pairs = []
    for device in range(XL * NZ * CO * NY * XH):
        xl, z, core, y, xh = place(device)
        there = number(xl ^ dxl, (z + dz) % NZ, core ^ dcore, (y + dy) % NY, xh ^ dxh)
        pairs.append((device, there))
    return lax.ppermute(value, AXES, pairs)


def coordinates():
    arc, col = lax.axis_index("arc"), lax.axis_index("col")
    xl, z, core = arc // (NZ * CO), (arc // CO) % NZ, arc % CO
    return xl, z, core, col // XH, col % XH


def scan_kernel(
    lengths_hbm, propagate_hbm, sight_hbm, weights_hbm, force_hbm,
    pack, coef, flat,
    lengths, propagate, sight, weights, keep, last, sems,
):
    loads = [
        pltpu.make_async_copy(force_hbm, flat, sems.at[0]),
        pltpu.make_async_copy(lengths_hbm, lengths, sems.at[1]),
        pltpu.make_async_copy(propagate_hbm, propagate, sems.at[2]),
        pltpu.make_async_copy(sight_hbm, sight, sems.at[3]),
        pltpu.make_async_copy(weights_hbm, weights, sems.at[4]),
    ]
    for load in loads:
        load.start()
    rank = lax.axis_index("arc")

    def clear(t, _):
        keep[t] = 1.0
        return 0

    lax.fori_loop(0, EPOCHS, clear, 0)
    loads[1].wait()

    def mark(arc, start):
        local = start - rank * EPOCHS

        @pl.when((local >= 0) & (local < EPOCHS))
        def _():
            keep[local] = 0.0

        return start + lengths[arc]

    lax.fori_loop(0, lengths.shape[0], mark, jnp.int32(0))
    lane = lax.broadcasted_iota(jnp.int32, (1, 256), 1)
    rows = tuple((lane == 192 + i).astype(jnp.float32) for i in range(6))
    loads[2].wait()
    loads[3].wait()
    loads[4].wait()

    def step(t, rows):
        live = keep[t]
        kicked = []
        for i in range(6):
            total = propagate[i, 0, t] * rows[0]
            for j in range(1, 6):
                total = total + propagate[i, j, t] * rows[j]
            kick = jnp.where(lane == (i % 3) * EPOCHS + t, 0.5 if i < 3 else 1.0, 0.0)
            kicked.append(live * total + kick)
        seen = sight[0, t] * kicked[0]
        for i in range(1, 6):
            seen = seen + sight[i, t] * kicked[i]
        coef[pl.ds(t, 1), :] = jnp.where(lane == 200, weights[t] / EVERY, seen)
        return tuple(kicked)

    rows = lax.fori_loop(0, EPOCHS, step, rows, unroll=4)
    last[...] = jnp.zeros_like(last)
    for i in range(6):
        last[i : i + 1, :] = rows[i]
    loads[0].wait()
    pack[:, :WIDE] = jnp.dot(
        last[:, : 3 * EPOCHS],
        flat[...].reshape(3 * EPOCHS, WIDE),
        precision=HIGH,
        preferred_element_type=jnp.float32,
    )
    pack[:, WIDE:] = last[:, 128:]


def scan(lengths, propagate, sight, weights, force):
    return pl.pallas_call(
        scan_kernel,
        out_shape=(
            jax.ShapeDtypeStruct((8, WIDE + 128), jnp.float32),
            jax.ShapeDtypeStruct((EPOCHS, 256), jnp.float32),
            jax.ShapeDtypeStruct(force.shape, jnp.float32),
        ),
        in_specs=[HBM] * 5,
        out_specs=(VMEM, VMEM, VMEM),
        scratch_shapes=[
            pltpu.SMEM(lengths.shape, jnp.int32),
            pltpu.SMEM(propagate.shape, jnp.float32),
            pltpu.SMEM(sight.shape, jnp.float32),
            pltpu.SMEM(weights.shape, jnp.float32),
            pltpu.SMEM((EPOCHS,), jnp.float32),
            pltpu.VMEM((8, 256), jnp.float32),
            pltpu.SemaphoreType.DMA((5,)),
        ],
        compiler_params=pltpu.CompilerParams(vmem_limit_bytes=WHOLE),
        name="scan",
    )(lengths, propagate, sight, weights, force)


def local_kernel(coef, flat, design):
    design[...] = jnp.dot(
        coef[:, : 3 * EPOCHS],
        flat[...].reshape(3 * EPOCHS, WIDE),
        precision=HIGH,
        preferred_element_type=jnp.float32,
    )


def local_design(coef, flat):
    return pl.pallas_call(
        local_kernel,
        out_shape=jax.ShapeDtypeStruct((EPOCHS, WIDE), jnp.float32),
        in_specs=[VMEM, VMEM],
        out_specs=VMEM,
        compiler_params=pltpu.CompilerParams(vmem_limit_bytes=16 * MIB),
        cost_estimate=pl.CostEstimate(flops=300_000_000, bytes_accessed=2_000_000, transcendentals=0),
        name="local",
    )(coef, flat)


def apply(matrix, state):
    total = matrix[:, 0:1] * state[0:1, :]
    for j in range(1, 6):
        total = total + matrix[:, j : j + 1] * state[j : j + 1, :]
    return total


def design_kernel(one, two, three, coef, local, design, keep, cross, weighted):
    state = three[:, :WIDE]
    for earlier in (two, one):
        state = apply(earlier[:, WIDE + 64 : WIDE + 70], state) + earlier[:, :WIDE]
    full = local[...] + apply(coef[:, 192:198], state)
    design[...] = full
    weighted[...] = full * coef[:, 200:201]
    _, _, _, y, xh = coordinates()
    for dy in range(NY):
        for dxh, out in enumerate((keep, cross)):
            slot = lax.rem(y + dy, NY) * XH + lax.rem(xh + dxh, XH)
            out[dy] = weighted[pl.ds(pl.multiple_of(slot * SLOTS, SLOTS), SLOTS), :]


def full_design(one, two, three, coef, local):
    pieces = jax.ShapeDtypeStruct((NY, SLOTS, WIDE), jnp.float32)
    return pl.pallas_call(
        design_kernel,
        out_shape=(jax.ShapeDtypeStruct((EPOCHS, WIDE), jnp.float32), pieces, pieces),
        in_specs=[VMEM] * 5,
        out_specs=(VMEM, VMEM, VMEM),
        scratch_shapes=[pltpu.VMEM((EPOCHS, WIDE), jnp.float32)],
        compiler_params=pltpu.CompilerParams(vmem_limit_bytes=16 * MIB),
        name="design",
    )(one, two, three, coef, local)


def pair_kernel(first, second, *outs):
    for i, out in enumerate(outs):
        out[0] = first[i]
        out[1] = second[i]


def pair(first, second):
    out = jax.ShapeDtypeStruct((2,) + first.shape[1:], jnp.float32)
    return pl.pallas_call(
        pair_kernel,
        out_shape=(out,) * first.shape[0],
        in_specs=[VMEM, VMEM],
        out_specs=(VMEM,) * first.shape[0],
        compiler_params=pltpu.CompilerParams(vmem_limit_bytes=16 * MIB),
        cost_estimate=pl.CostEstimate(flops=5_000_000_000, bytes_accessed=1_000_000, transcendentals=0),
        name="pair",
    )(first, second)


def choose_kernel(order, *refs):
    pieces, out, blocks = refs[:4], refs[4], refs[5]
    _, _, core, y, xh = coordinates()
    for dy in range(NY):
        for dxh in range(XH):
            col = lax.rem(y + dy, NY) * XH + lax.rem(xh + dxh, XH)
            for j in range(4):
                blocks[4 * col + j] = pieces[dy][dxh, :, BLOCK * j : BLOCK * (j + 1)]
    for chip in range(XL * NZ):
        for dcore in range(CO):
            out[chip, dcore] = blocks[order[chip * CO + lax.rem(core + dcore, CO)]]


def choose(order, pieces):
    return pl.pallas_call(
        choose_kernel,
        out_shape=jax.ShapeDtypeStruct((XL * NZ, CO, SLOTS, BLOCK), jnp.float32),
        in_specs=[SMEM] + [VMEM] * 4,
        out_specs=VMEM,
        scratch_shapes=[pltpu.VMEM((32, SLOTS, BLOCK), jnp.float32)],
        compiler_params=pltpu.CompilerParams(vmem_limit_bytes=16 * MIB),
        name="choose",
    )(order, *pieces)


def turn_kernel(pieces, out, gathered):
    xl, z, _, _, _ = coordinates()
    for dcore in range(CO):
        for dxl in range(XL):
            for dz in range(NZ):
                chip = lax.rem(xl + dxl, XL) * NZ + lax.rem(z + dz, NZ)
                start = SLOTS * (dxl * NZ + dz)
                gathered[start : start + SLOTS, :BLOCK] = pieces[chip, dcore]
        out[BLOCK * dcore : BLOCK * (dcore + 1), :] = jnp.transpose(gathered[...])[:BLOCK]


def turn(pieces):
    return pl.pallas_call(
        turn_kernel,
        out_shape=jax.ShapeDtypeStruct((CO * BLOCK, 128), jnp.float32),
        in_specs=[VMEM],
        out_specs=VMEM,
        scratch_shapes=[pltpu.VMEM((128, 512), jnp.float32)],
        compiler_params=pltpu.CompilerParams(vmem_limit_bytes=16 * MIB),
        name="turn",
    )(pieces)


def split(value):
    high = value.astype(jnp.bfloat16)
    return high, (value - high.astype(jnp.float32)).astype(jnp.bfloat16)


def stack_kernel(*refs):
    left, out = refs[:-1], refs[-1]
    depth = 128 * len(left)
    for j, shard in enumerate(left):
        high, low = split(shard[...])
        for part, value in enumerate((high, low, high)):
            out[:, depth * part + 128 * j : depth * part + 128 * (j + 1)] = value


def stack_early(left):
    return pl.pallas_call(
        stack_kernel,
        out_shape=jax.ShapeDtypeStruct((CO * BLOCK, 3 * 128 * len(left)), jnp.bfloat16),
        in_specs=[VMEM] * len(left),
        out_specs=VMEM,
        compiler_params=pltpu.CompilerParams(vmem_limit_bytes=12 * MIB),
        name="stack",
    )(*left)


def pick_kernel(*refs):
    left, out = refs[:-1], refs[-1]
    lanes = slice(SLOTS * LATE[0], SLOTS * (LATE[-1] + 1))
    value = jnp.concatenate([shard[:, lanes] for shard in left], axis=1)
    high = value.astype(jnp.bfloat16).astype(jnp.float32)
    out[...] = jnp.concatenate([high, value - high, high], axis=1).astype(jnp.bfloat16)


def pick_late(left):
    return pl.pallas_call(
        pick_kernel,
        out_shape=jax.ShapeDtypeStruct((CO * BLOCK, 3 * PICK), jnp.bfloat16),
        in_specs=[VMEM] * len(left),
        out_specs=VMEM,
        compiler_params=pltpu.CompilerParams(vmem_limit_bytes=12 * MIB),
        name="pick",
    )(*left)


def bring_kernel(*refs):
    half = len(refs) // 2
    for source, target in zip(refs[:half], refs[half:]):
        target[...] = source[...]


def bring(values):
    return pl.pallas_call(
        bring_kernel,
        out_shape=tuple(jax.ShapeDtypeStruct(value.shape, value.dtype) for value in values),
        in_specs=[VMEM] * len(values),
        out_specs=(VMEM,) * len(values),
        compiler_params=pltpu.CompilerParams(vmem_limit_bytes=12 * MIB),
        name="bring",
    )(*values)


def slot_rows(dy, dxh):
    _, _, _, y, xh = coordinates()
    slot = lax.rem(y + dy, NY) * XH + lax.rem(xh + dxh, XH)
    return pl.ds(pl.multiple_of(slot * SLOTS, SLOTS), SLOTS)


def early_kernel(lo, hi, left, *refs):
    right, outs, stacked = refs[:12], refs[12:14], refs[14]
    depth = 128 * len(EARLY)
    none = jnp.zeros((SLOTS * len(LATE), hi - lo), jnp.float32)
    for j, place in enumerate(EARLY):
        rows = slot_rows(*place)
        chunk = [block[rows, lo:hi] for block in right]
        high, low = split(jnp.concatenate(chunk[: LATE[0]] + [none] + chunk[LATE[0] :], axis=0))
        for part, value in enumerate((high, high, low)):
            stacked[depth * part + 128 * j : depth * part + 128 * (j + 1), :] = value
    for i, out in enumerate(outs):
        out[...] = jnp.dot(
            left[BLOCK * i : BLOCK * (i + 1), :], stacked[...], preferred_element_type=jnp.float32
        )


def early_product(left, right, lo, hi):
    out = jax.ShapeDtypeStruct((BLOCK, hi - lo), jnp.float32)
    depth = 128 * len(EARLY)
    return pl.pallas_call(
        functools.partial(early_kernel, lo, hi),
        out_shape=(out, out),
        in_specs=[VMEM] * 13,
        out_specs=(VMEM, VMEM),
        scratch_shapes=[pltpu.VMEM((3 * depth, hi - lo), jnp.bfloat16)],
        compiler_params=pltpu.CompilerParams(vmem_limit_bytes=14 * MIB),
        cost_estimate=pl.CostEstimate(
            flops=12 * BLOCK * depth * (hi - lo), bytes_accessed=14_000_000, transcendentals=0
        ),
        name="early",
    )(left, *right)


def late_kernel(lo, hi, first, second, picked, *refs):
    right, sums, outs, across, stacked = refs[:16], refs[16:18], refs[18:20], refs[20], refs[21]
    for j, (place, shard) in enumerate(zip(LAST, (first, second))):
        high, low = split(shard[...])
        for part, value in enumerate((high, low, high)):
            across[:, DEEP * part + 128 * j : DEEP * part + 128 * (j + 1)] = value
        rows = slot_rows(*place)
        high, low = split(jnp.concatenate([block[rows, lo:hi] for block in right], axis=0))
        for part, value in enumerate((high, high, low)):
            stacked[DEEP * part + 128 * j : DEEP * part + 128 * (j + 1), :] = value
    across[:, 3 * DEEP :] = picked[...]
    pieces = [right[i][slot_rows(*place), lo:hi] for place in EARLY for i in LATE]
    high, low = split(jnp.concatenate(pieces, axis=0))
    for part, value in enumerate((high, high, low)):
        stacked[3 * DEEP + PICK * part : 3 * DEEP + PICK * (part + 1), :] = value
    for i, out in enumerate(outs):
        out[...] = sums[i][...] + jnp.dot(
            across[BLOCK * i : BLOCK * (i + 1), :], stacked[...], preferred_element_type=jnp.float32
        )


def late_product(left, picked, right, lo, hi, sums):
    out = jax.ShapeDtypeStruct((BLOCK, hi - lo), jnp.float32)
    depth = 3 * (DEEP + PICK)
    return pl.pallas_call(
        functools.partial(late_kernel, lo, hi),
        out_shape=(out, out),
        in_specs=[VMEM] * 21,
        out_specs=(VMEM, VMEM),
        scratch_shapes=[
            pltpu.VMEM((CO * BLOCK, depth), jnp.bfloat16),
            pltpu.VMEM((depth, hi - lo), jnp.bfloat16),
        ],
        compiler_params=pltpu.CompilerParams(vmem_limit_bytes=14 * MIB),
        cost_estimate=pl.CostEstimate(
            flops=4 * BLOCK * depth * (hi - lo), bytes_accessed=14_000_000, transcendentals=0
        ),
        name="late",
    )(*left, picked, *right, *sums)


def finish_kernel(lo, hi, mine, passed, *refs):
    out, total, sem = refs[-3:]
    total[...] = mine[...] + passed[...]
    copy = pltpu.make_async_copy(total, out.at[:, lo:hi], sem)
    copy.start()
    copy.wait()


def finish(mine, passed, lo, hi, whole=None):
    given = () if whole is None else (whole,)
    return pl.pallas_call(
        functools.partial(finish_kernel, lo, hi),
        out_shape=jax.ShapeDtypeStruct((BLOCK, WIDE), jnp.float32),
        in_specs=[VMEM, VMEM] + [HBM] * len(given),
        out_specs=HBM,
        scratch_shapes=[pltpu.VMEM((BLOCK, hi - lo), jnp.float32), pltpu.SemaphoreType.DMA],
        input_output_aliases={2: 0} if given else {},
        compiler_params=pltpu.CompilerParams(vmem_limit_bytes=16 * MIB),
        name="finish",
    )(mine, passed, *given)


def shift_arc(value, step):
    arcs, cols = XL * NZ * CO, NY * XH
    pairs = [
        (arc * cols + col, (arc + step) * cols + col)
        for arc in range(arcs - step)
        for col in range(cols)
    ]
    return lax.ppermute(value, AXES, pairs)


def body(force, propagate, sight, weights, lengths, order):
    tie = lax.optimization_barrier
    pack, coef, flat = scan(lengths, propagate, sight, weights, force)
    before = [shift_arc(pack, step) for step in (1, 2, 3)]
    design, keep, cross = full_design(*before, coef, local_design(coef, flat))
    own, far = {0: design}, {}
    got, beside = tie((send(cross, dxh=1), own[0]))
    own[-1], own[1] = send(own[0], dz=1), send(own[0], dz=-1)
    to = pair(keep, got)
    rows = [to[0], send(to[3], dy=-1), send(to[2], dy=2), send(to[1], dy=1)]
    rows, own = tie((rows, own))
    own[-2], own[2] = send(own[-1], dz=1), send(own[1], dz=-1)
    third = send(own[-2], dz=1), send(own[2], dz=-1)
    far[0], beside = tie((send(beside, dxl=1), own[1]))
    second = send(beside, dxl=1)
    chosen = choose(order, rows)
    same_core = [[chip * CO + core for chip in range(XL * NZ)] for core in range(CO)]
    column = lax.all_to_all(chosen, "arc", 0, 0, axis_index_groups=same_core, tiled=True)
    column, own, far = tie((column, own, far))
    (own[-3], own[3]), far[1] = third, second
    near, across = {0: turn(column)}, {}
    near[-1], near[1], across[0] = send(near[0], dy=1), send(near[0], dy=-1), send(near[0], dxh=1)
    own[-3], own[3], far[0], far[1] = tie((own[-3], own[3], far[0], far[1]))
    far[-1], own[4] = send(far[0], dz=1), send(own[3], dz=-1)
    far[-1], near[-1], near[1], own[4] = tie((far[-1], near[-1], near[1], own[4]))
    across[0], beside = tie((across[0], own[3]))
    far[3] = send(beside, dxl=1)
    across[-1], across[1] = send(across[0], dy=1), send(across[0], dy=-1)
    across[-1], beside = tie((across[-1], near[-1]))
    near[2] = send(beside, dy=1)
    far[-2], far[2] = send(far[-1], dz=1), send(far[1], dz=-1)
    across[1], far[3] = tie((across[1], far[3]))
    across[2] = send(across[1], dy=-1)
    left = [(near, across)[dxh][dy if dy <= 2 else dy - 4] for dy, dxh in EARLY]
    stacked, picked, far[-2] = tie((stack_early(left), pick_late(left), far[-2]))
    far[-3], far[4] = send(far[-2], dz=1), send(own[4], dxl=1)
    own[3], own[-3], far[1] = bring((own[3], own[-3], far[1]))
    right = [group[d if d <= 4 else d - 8] for group in (own, far) for d in range(NZ)]
    cuts = ((0, 1280), (1280, WIDE))
    ready = right[: LATE[0]] + right[LATE[-1] + 1 :]
    sums = [early_product(stacked, ready, *cut) for cut in cuts]
    late = [right[i] for i in LATE]
    last, late, sums = tie(([near[2], across[2]], late, sums))
    right[LATE[0] : LATE[-1] + 1] = late
    mine_a, other_a = late_product(last, picked, right, *cuts[0], sums[0])
    passed_a = send(other_a, dcore=1)
    mine_b, other_b = late_product(last, picked, right, *cuts[1], sums[1])
    passed_b = send(other_b, dcore=1)
    whole = finish(mine_a, passed_a, *cuts[0])
    return finish(mine_b, passed_b, *cuts[1], whole)


def solution(mesh):
    in_specs = (P(None, "arc", "col"), P(None, None, "arc"), P(None, "arc"), P("arc"), P(), P())
    out_specs = P("arc", "col")
    return jax.shard_map(body, mesh=mesh, in_specs=in_specs, out_specs=out_specs, check_vma=False)
```

time: 422 us -> 131 us (0.31)
  blocking collectives: 183 us -> 0 us
  matrix products: 74.6 us -> 0 us
  waiting for transfers between devices: 112 us -> 47.7 us
  starting transfers between devices: 0.27 us -> 49.3 us
  Pallas kernels: 0 us -> 30.6 us
  local copies, waits for them, and re-layouts: 23.8 us -> 2.21 us
  between operations: 13.8 us -> 0.43 us
  other arithmetic: 10.3 us -> 0 us
    all_to_all x1 -> x0, blocking collectives: 146 us -> none  [body(): lax.all_to_all(grouped, 'arc', split_axis=1, concat_axis=0, tiled=True)]
    all_gather x3 -> x0, waiting for transfers between devices: 112 us -> none  [the longest x1 72.1 us: body(): full = lax.all_gather(design, 'col', axis=1, tiled=True)]
    dot_general x59 -> x0, matrix products: 74.6 us -> none  [the longest x1 32.6 us: contract_rows(): lax.dot_general(left, right, (((0,), (0,)), ((), ())), precision=HIGH, pr...]
    ppermute x0 -> x31, starting transfers between devices: none -> 43.8 us  [the longest x28 32.6 us: send(): return lax.ppermute(value, AXES, pairs)]
    ppermute x0 -> x31, waiting for transfers between devices: none -> 41 us  [the longest x28 39.2 us: send(): return lax.ppermute(value, AXES, pairs)]
    all_gather x1 -> x0, blocking collectives: 37.1 us -> none  [prefix(): pieces = jax.tree.map(lambda part: lax.all_gather(part, axis), value)]
    pallas_call x0 -> x15, Pallas kernels: none -> 30.6 us  [the longest x2 9.68 us: early_product(): pl.pallas_call(functools.partial(early_kernel, lo, hi), out_shape=(out, o...]
    reshape x2 -> x0, local copies, waits for them, and re-layouts: 12.6 us -> none  [body(): weighted.reshape(epoch_dev, arc_count, width_blk)]
  transfers between devices with their start and end apart: 3 -> 32, of which waited for: 3 -> 14; matrix products, arithmetic and copies ran while one was open for 7% -> 0% of each run, Pallas kernels for 0% -> 15%
where the time goes in v1:
time: 131 us; the launch traced here: 130 us
  starting transfers between devices  49.3 us (38%)
  waiting for transfers between devices  47.7 us (36%)
  Pallas kernels  30.6 us (23%)
  local copies, waits for them, and re-layouts  2.21 us (2%)
    ppermute x28, waiting for transfers between devices, send(): return lax.ppermute(value, AXES, pairs)  39.2 us
    ppermute x28, starting transfers between devices, send(): return lax.ppermute(value, AXES, pairs)  32.6 us
    ppermute x3, starting transfers between devices, shift_arc(): return lax.ppermute(value, AXES, pairs)  11.2 us
    pallas_call x2, Pallas kernels, early_product(): pl.pallas_call(functools.partial(early_kernel, lo, hi), out_shape=(out, o...  9.68 us
    all_to_all x1, waiting for transfers between devices, body(): lax.all_to_all(chosen, 'arc', 0, 0, axis_index_groups=same_core, tiled=True)  6.66 us
    pallas_call x2, Pallas kernels, late_product(): pl.pallas_call(functools.partial(late_kernel, lo, hi), out_shape=(out, ou...  6.59 us
    all_to_all x1, starting transfers between devices, body(): lax.all_to_all(chosen, 'arc', 0, 0, axis_index_groups=same_core, tiled=True)  5.46 us
    pallas_call x1, Pallas kernels, scan(): pl.pallas_call(scan_kernel, out_shape=(jax.ShapeDtypeStruct((8, WIDE + 12...  5.05 us
  transfers between devices with their start and end apart: 32, of which 14 were waited for; matrix products, arithmetic and copies ran while one was open for 0% of the time, Pallas kernels for 15%

profile of v1, /device:TPU:3, one launch (start us, length us, event | category | flops | bytes accessed | tf_op | source)
XLA Modules:
  0.0 130.2 jit_solution(16266232326322343108)
XLA Ops:
  0.0 5.0 %scan.1 = (f32[8,2048]{1,0:T(8,128)}, f32[64,256]{1,0:T(8,128)}, f32[3,64,1920]{2,1,0:T(8,128)}) custom-call(s32[32]{0:T(128)} %lengths_hbm.1, f32[6,6,64]{2,1,0:T(8,128)} %propagate_hbm.1, f32[6,64]{1,0:T(8,128)} %sight_hbm.1, f32[64]{0:T(128)} %weights_hbm.1, f32[3,64,1920]{2,1,0:T(8,128)} %force_hbm.1), custom_call_target="tpu_custom_call" | custom-call | tf_op jit(solution)/shard_map/scan/pallas_call | solution.py:126
  5.1 4.1 %collective-permute-start = (f32[8,2048]{1,0:T(8,128)}, f32[8,2048]{1,0:T(8,128)S(1)}, u32[]{:S(2)}, u32[]{:S(2)}) collective-permute-start(f32[8,2048]{1,0:T(8,128)} %get-tuple-element.71), channel_id=1, source_target_pairs={{0,8},{1,9},{2,10},{3,11},{4,12},{5,13},{6,14},{7,15},{8,16},{9,17... | collective-permute-start | bytes 196616 | tf_op jit(solution)/shard_map/ppermute | solution.py:441
  9.2 3.5 %collective-permute-start.1 = (f32[8,2048]{1,0:T(8,128)}, f32[8,2048]{1,0:T(8,128)S(1)}, u32[]{:S(2)}, u32[]{:S(2)}) collective-permute-start(f32[8,2048]{1,0:T(8,128)} %get-tuple-element.71), channel_id=1, source_target_pairs={{0,16},{1,17},{2,18},{3,19},{4,20},{5,21},{6,22},{7,23},{8,24},{9,... | collective-permute-start | bytes 196616 | tf_op jit(solution)/shard_map/ppermute | solution.py:441
  12.7 3.6 %collective-permute-start.2 = (f32[8,2048]{1,0:T(8,128)}, f32[8,2048]{1,0:T(8,128)S(1)}, u32[]{:S(2)}, u32[]{:S(2)}) collective-permute-start(f32[8,2048]{1,0:T(8,128)} %get-tuple-element.71), channel_id=1, source_target_pairs={{0,24},{1,25},{2,26},{3,27},{4,28},{5,29},{6,30},{7,31},{8,32},{9,... | collective-permute-start | bytes 196616 | tf_op jit(solution)/shard_map/ppermute | solution.py:441
  19.5 1.8 %collective-permute-done.2.three = f32[8,2048]{1,0:T(8,128)S(1)} collective-permute-done((f32[8,2048]{1,0:T(8,128)}, f32[8,2048]{1,0:T(8,128)S(1)}, u32[]{:S(2)}, u32[]{:S(2)}) %collective-permute-start.2) | collective-permute-done | bytes 65568 | tf_op jit(solution)/shard_map/ppermute | solution.py:441
  21.8 2.0 %collective-permute-start.3 = (f32[4,8,1920]{2,1,0:T(8,128)S(1)}, f32[4,8,1920]{2,1,0:T(8,128)S(1)}, u32[]{:S(2)}, u32[]{:S(2)}) collective-permute-start(f32[4,8,1920]{2,1,0:T(8,128)S(1)} %get-tuple-element.75), channel_id=1, source_target_pairs={{0,1},{1,0},{2,3},{3,2},{4,5},{5,4},{6,7},{7,6},{8,9},{9,8},{10,11... | collective-permute-start | bytes 737288 | tf_op jit(solution)/shard_map/ppermute | solution.py:48
  24.8 1.8 %collective-permute-start.8 = (f32[64,1920]{1,0:T(8,128)S(1)}, f32[64,1920]{1,0:T(8,128)S(1)}, u32[]{:S(2)}, u32[]{:S(2)}) collective-permute-start(f32[64,1920]{1,0:T(8,128)S(1)} %get-tuple-element.108.refs_0_), channel_id=1, source_target_pairs={{0,112},{1,113},{2,114},{3,115},{4,116},{5,117},{6,118},{7,119},{8... | collective-permute-start | bytes 1474568 | tf_op jit(solution)/shard_map/ppermute | solution.py:48
  26.5 4.8 %collective-permute-done.3.second = f32[4,8,1920]{2,1,0:T(8,128)S(1)} collective-permute-done((f32[4,8,1920]{2,1,0:T(8,128)S(1)}, f32[4,8,1920]{2,1,0:T(8,128)S(1)}, u32[]{:S(2)}, u32[]{:S(2)}) %collective-permute-start.3) | collective-permute-done | bytes 245792 | tf_op jit(solution)/shard_map/ppermute | solution.py:48
  31.3 2.8 %collective-permute-start.4 = (f32[2,8,1920]{2,1,0:T(8,128)S(1)}, f32[2,8,1920]{2,1,0:T(8,128)S(1)}, u32[]{:S(2)}, u32[]{:S(2)}) collective-permute-start(f32[2,8,1920]{2,1,0:T(8,128)S(1)} %get-tuple-element.79), channel_id=1, source_target_pairs={{0,6},{1,7},{2,0},{3,1},{4,2},{5,3},{6,4},{7,5},{8,14},{9,15},{10,... | collective-permute-start | bytes 368648 | tf_op jit(solution)/shard_map/ppermute | solution.py:48
  35.2 3.8 %collective-permute-done.4.refs_1_ = f32[2,8,1920]{2,1,0:T(8,128)S(1)} collective-permute-done((f32[2,8,1920]{2,1,0:T(8,128)S(1)}, f32[2,8,1920]{2,1,0:T(8,128)S(1)}, u32[]{:S(2)}, u32[]{:S(2)}) %collective-permute-start.4) | collective-permute-done | bytes 122912 | tf_op jit(solution)/shard_map/ppermute | solution.py:48
  39.9 3.6 %collective-permute-done.6.refs_3_ = f32[2,8,1920]{2,1,0:T(8,128)S(1)} collective-permute-done((f32[2,8,1920]{2,1,0:T(8,128)S(1)}, f32[2,8,1920]{2,1,0:T(8,128)S(1)}, u32[]{:S(2)}, u32[]{:S(2)}) %collective-permute-start.6) | collective-permute-done | bytes 122912 | tf_op jit(solution)/shard_map/ppermute | solution.py:48
  43.5 2.7 %collective-permute-start.10 = (f32[64,1920]{1,0:T(8,128)S(1)}, f32[64,1920]{1,0:T(8,128)S(1)}, u32[]{:S(2)}, u32[]{:S(2)}) collective-permute-start(f32[64,1920]{1,0:T(8,128)S(1)} %collective-permute-done.8.refs_1_), channel_id=1, source_target_pairs={{0,112},{1,113},{2,114},{3,115},{4,116},{5,117},{6,118},{7,119},{8... | collective-permute-start | bytes 1474568 | tf_op jit(solution)/shard_map/ppermute | solution.py:48
  46.2 1.6 %choose.1 = f32[16,2,8,480]{3,2,1,0:T(8,128)} custom-call(s32[32]{0:T(128)S(1)} %copy-done.2, f32[2,8,1920]{2,1,0:T(8,128)S(1)} %get-tuple-element.82.refs_0_, f32[2,8,1920]{2,1,0:T(8,128)S(1)} %collective-permute-done.4.refs_1_, f32[2,8,1920]{2,1,0:T(8,128)S(1)} %collective-permute-done.5.refs_2_, f32[2,8,1920]{2,1,0:T(8,128)S(1)} %collective-permute-done.6.refs_3_), custom_call_target="tpu_custom_call" | custom-call | tf_op jit(solution)/shard_map/choose/pallas_call | solution.py:237
  47.8 5.5 %all-to-all-start = ((f32[16,2,8,480]{3,2,1,0:T(8,128)}), f32[16,2,8,480]{3,2,1,0:T(8,128)S(1)}, u32[]{:S(2)}, u32[]{:S(2)}) async-start(f32[16,2,8,480]{3,2,1,0:T(8,128)} %choose.1), calls=%async_computation | async-start | bytes 1048576 | tf_op jit(solution)/shard_map/all_to_all | solution.py:461
  53.4 3.6 %collective-permute-done.9.refs_6_ = f32[64,1920]{1,0:T(8,128)S(1)} collective-permute-done((f32[64,1920]{1,0:T(8,128)S(1)}, f32[64,1920]{1,0:T(8,128)S(1)}, u32[]{:S(2)}, u32[]{:S(2)}) %collective-permute-start.9) | collective-permute-done | bytes 491552 | tf_op jit(solution)/shard_map/ppermute | solution.py:48
  57.1 3.0 %collective-permute-start.14 = (f32[64,1920]{1,0:T(8,128)S(1)}, f32[64,1920]{1,0:T(8,128)}, u32[]{:S(2)}, u32[]{:S(2)}) collective-permute-start(f32[64,1920]{1,0:T(8,128)S(1)} %collective-permute-done.10.refs_2_), channel_id=1, source_target_pairs={{0,112},{1,113},{2,114},{3,115},{4,116},{5,117},{6,118},{7,119},{8... | collective-permute-start | bytes 1474568 | tf_op jit(solution)/shard_map/ppermute | solution.py:48
  60.1 6.7 %all-to-all-done.pieces = f32[16,2,8,480]{3,2,1,0:T(8,128)S(1)} async-done(((f32[16,2,8,480]{3,2,1,0:T(8,128)}), f32[16,2,8,480]{3,2,1,0:T(8,128)S(1)}, u32[]{:S(2)}, u32[]{:S(2)}) %all-to-all-start) | async-done | bytes 491552 | tf_op jit(solution)/shard_map/all_to_all | solution.py:461
  67.0 1.9 %collective-permute-start.12 = (f32[960,128]{1,0:T(8,128)S(1)}, f32[960,128]{1,0:T(8,128)S(1)}, u32[]{:S(2)}, u32[]{:S(2)}) collective-permute-start(f32[960,128]{1,0:T(8,128)S(1)} %turn.1.refs_0_), channel_id=1, source_target_pairs={{0,1},{1,0},{2,3},{3,2},{4,5},{5,4},{6,7},{7,6},{8,9},{9,8},{10,11... | collective-permute-start | bytes 1474568 | tf_op jit(solution)/shard_map/ppermute | solution.py:48
  69.8 1.7 %collective-permute-start.19 = (f32[960,128]{1,0:T(8,128)S(1)}, f32[960,128]{1,0:T(8,128)S(1)}, u32[]{:S(2)}, u32[]{:S(2)}) collective-permute-start(f32[960,128]{1,0:T(8,128)S(1)} %turn.1.refs_0_), channel_id=1, source_target_pairs={{0,6},{1,7},{2,0},{3,1},{4,2},{5,3},{6,4},{7,5},{8,14},{9,15},{10,... | collective-permute-start | bytes 1474568 | tf_op jit(solution)/shard_map/ppermute | solution.py:48
  71.6 7.5 %collective-permute-done.13.refs_1_ = f32[64,1920]{1,0:T(8,128)} collective-permute-done((f32[64,1920]{1,0:T(8,128)S(1)}, f32[64,1920]{1,0:T(8,128)}, u32[]{:S(2)}, u32[]{:S(2)}) %collective-permute-start.13) | collective-permute-done | bytes 491552 | tf_op jit(solution)/shard_map/ppermute | solution.py:48
  79.0 2.7 %collective-permute-start.20 = (f32[64,1920]{1,0:T(8,128)}, f32[64,1920]{1,0:T(8,128)S(1)}, u32[]{:S(2)}, u32[]{:S(2)}) collective-permute-start(f32[64,1920]{1,0:T(8,128)} %collective-permute-done.14.refs_0_), channel_id=1, source_target_pairs={{0,112},{1,113},{2,114},{3,115},{4,116},{5,117},{6,118},{7,119},{8... | collective-permute-start | bytes 1474568 | tf_op jit(solution)/shard_map/ppermute | solution.py:48
  81.7 2.7 %collective-permute-start.22 = (f32[960,128]{1,0:T(8,128)S(1)}, f32[960,128]{1,0:T(8,128)S(1)}, u32[]{:S(2)}, u32[]{:S(2)}) collective-permute-start(f32[960,128]{1,0:T(8,128)S(1)} %collective-permute-done.12.refs_1_), channel_id=1, source_target_pairs={{0,6},{1,7},{2,0},{3,1},{4,2},{5,3},{6,4},{7,5},{8,14},{9,15},{10,... | collective-permute-start | bytes 1474568 | tf_op jit(solution)/shard_map/ppermute | solution.py:48
  84.7 7.0 %collective-permute-done.17.refs_11_.refs_15_ = f32[64,1920]{1,0:T(8,128)S(1)} collective-permute-done((f32[64,1920]{1,0:T(8,128)S(1)}, f32[64,1920]{1,0:T(8,128)S(1)}, u32[]{:S(2)}, u32[]{:S(2)}) %collective-permute-start.17) | collective-permute-done | bytes 491552 | tf_op jit(solution)/shard_map/ppermute | solution.py:48
  92.5 1.9 %collective-permute-start.28 = (f32[64,1920]{1,0:T(8,128)}, f32[64,1920]{1,0:T(8,128)S(1)}, u32[]{:S(2)}, u32[]{:S(2)}) collective-permute-start(f32[64,1920]{1,0:T(8,128)} %collective-permute-done.15.refs_2_), channel_id=1, source_target_pairs={{0,112},{1,113},{2,114},{3,115},{4,116},{5,117},{6,118},{7,119},{8... | collective-permute-start | bytes 1474568 | tf_op jit(solution)/shard_map/ppermute | solution.py:48
  99.3 4.1 %collective-permute-done.26.refs_14_ = f32[64,1920]{1,0:T(8,128)S(1)} collective-permute-done((f32[64,1920]{1,0:T(8,128)S(1)}, f32[64,1920]{1,0:T(8,128)S(1)}, u32[]{:S(2)}, u32[]{:S(2)}) %collective-permute-start.26) | collective-permute-done | bytes 491552 | tf_op jit(solution)/shard_map/ppermute | solution.py:48
  103.5 3.7 %early.3 = (f32[480,640]{1,0:T(8,128)S(1)}, f32[480,640]{1,0:T(8,128)S(1)}) custom-call(bf16[960,2304]{1,0:T(8,128)(2,1)S(1)} %stack.1.left, f32[64,1920]{1,0:T(8,128)S(1)} %get-tuple-element.108.refs_0_, f32[64,1920]{1,0:T(8,128)S(1)} %collective-permute-done.8.refs_1_, f32[64,1920]{1,0:T(8,128)S(1)} %collective-permute-done.10.refs_2_, ...), custom_call_target="tpu_custom_call" | custom-call | flops 2831155200 | bytes 14000000 | tf_op jit(solution)/shard_map/early/pallas_call | solution.py:357
  107.2 6.0 %early.2 = (f32[480,1280]{1,0:T(8,128)S(1)}, f32[480,1280]{1,0:T(8,128)S(1)}) custom-call(bf16[960,2304]{1,0:T(8,128)(2,1)S(1)} %stack.1.left, f32[64,1920]{1,0:T(8,128)S(1)} %get-tuple-element.108.refs_0_, f32[64,1920]{1,0:T(8,128)S(1)} %collective-permute-done.8.refs_1_, f32[64,1920]{1,0:T(8,128)S(1)} %collective-permute-done.10.refs_2_, ...), custom_call_target="tpu_custom_call" | custom-call | flops 5662310400 | bytes 14000000 | tf_op jit(solution)/shard_map/early/pallas_call | solution.py:357
  114.3 4.1 %late.3 = (f32[480,1280]{1,0:T(8,128)S(1)}, f32[480,1280]{1,0:T(8,128)S(1)}) custom-call(f32[960,128]{1,0:T(8,128)S(1)} %collective-permute-done.21.first, f32[960,128]{1,0:T(8,128)S(1)} %collective-permute-done.24.second, bf16[960,576]{1,0:T(8,128)(2,1)S(1)} %pick.1.picked, f32[64,1920]{1,0:T(8,128)S(1)} %get-tuple-element.108.refs_0_, ...), custom_call_target="tpu_custom_call" | custom-call | flops 3303014400 | bytes 14000000 | tf_op jit(solution)/shard_map/late/pallas_call | solution.py:395
  118.4 4.4 %collective-permute-start.30 = (f32[480,1280]{1,0:T(8,128)S(1)}, f32[480,1280]{1,0:T(8,128)S(1)}, u32[]{:S(2)}, u32[]{:S(2)}) collective-permute-start(f32[480,1280]{1,0:T(8,128)S(1)} %get-tuple-element.136), channel_id=1, source_target_pairs={{0,8},{1,9},{2,10},{3,11},{4,12},{5,13},{6,14},{7,15},{8,0},{9,1},... | collective-permute-start | bytes 7372808 | tf_op jit(solution)/shard_map/ppermute | solution.py:48
  122.7 2.5 %late.2 = (f32[480,640]{1,0:T(8,128)S(1)}, f32[480,640]{1,0:T(8,128)S(1)}) custom-call(f32[960,128]{1,0:T(8,128)S(1)} %collective-permute-done.21.first, f32[960,128]{1,0:T(8,128)S(1)} %collective-permute-done.24.second, bf16[960,576]{1,0:T(8,128)(2,1)S(1)} %pick.1.picked, f32[64,1920]{1,0:T(8,128)S(1)} %get-tuple-element.108.refs_0_, ...), custom_call_target="tpu_custom_call" | custom-call | flops 1651507200 | bytes 14000000 | tf_op jit(solution)/shard_map/late/pallas_call | solution.py:395
  125.4 1.7 %collective-permute-done.30.passed = f32[480,1280]{1,0:T(8,128)S(1)} collective-permute-done((f32[480,1280]{1,0:T(8,128)S(1)}, f32[480,1280]{1,0:T(8,128)S(1)}, u32[]{:S(2)}, u32[]{:S(2)}) %collective-permute-start.30) | collective-permute-done | bytes 2457632 | tf_op jit(solution)/shard_map/ppermute | solution.py:48
  127.0 1.7 %finish.2.refs_0_ = f32[480,1920]{1,0:T(8,128)} custom-call(f32[480,1280]{1,0:T(8,128)S(1)} %get-tuple-element.135.mine, f32[480,1280]{1,0:T(8,128)S(1)} %collective-permute-done.30.passed), custom_call_target="tpu_custom_call" | custom-call | tf_op jit(solution)/shard_map/finish/pallas_call | solution.py:422
  (53 shorter events, 16.3 us)
Async XLA Ops:
  5.1 14.5 %collective-permute-start = (f32[8,2048]{1,0:T(8,128)}, f32[8,2048]{1,0:T(8,128)S(1)}, u32[]{:S(2)}, u32[]{:S(2)}) collective-permute-start(f32[8,2048]{1,0:T(8,128)} %get-tuple-element.71), channel_id=1, source_target_pairs={{0,8},{1,9},{2,10},{3,11},{4,12},{5,13},{6,14},{7,15},{8,16},{9,17... | collective-permute-start | bytes 196616 | tf_op jit(solution)/shard_map/ppermute | solution.py:441
  9.2 10.4 %collective-permute-start.1 = (f32[8,2048]{1,0:T(8,128)}, f32[8,2048]{1,0:T(8,128)S(1)}, u32[]{:S(2)}, u32[]{:S(2)}) collective-permute-start(f32[8,2048]{1,0:T(8,128)} %get-tuple-element.71), channel_id=1, source_target_pairs={{0,16},{1,17},{2,18},{3,19},{4,20},{5,21},{6,22},{7,23},{8,24},{9,... | collective-permute-start | bytes 196616 | tf_op jit(solution)/shard_map/ppermute | solution.py:441
  12.7 8.6 %collective-permute-start.2 = (f32[8,2048]{1,0:T(8,128)}, f32[8,2048]{1,0:T(8,128)S(1)}, u32[]{:S(2)}, u32[]{:S(2)}) collective-permute-start(f32[8,2048]{1,0:T(8,128)} %get-tuple-element.71), channel_id=1, source_target_pairs={{0,24},{1,25},{2,26},{3,27},{4,28},{5,29},{6,30},{7,31},{8,32},{9,... | collective-permute-start | bytes 196616 | tf_op jit(solution)/shard_map/ppermute | solution.py:441
  21.8 9.5 %collective-permute-start.3 = (f32[4,8,1920]{2,1,0:T(8,128)S(1)}, f32[4,8,1920]{2,1,0:T(8,128)S(1)}, u32[]{:S(2)}, u32[]{:S(2)}) collective-permute-start(f32[4,8,1920]{2,1,0:T(8,128)S(1)} %get-tuple-element.75), channel_id=1, source_target_pairs={{0,1},{1,0},{2,3},{3,2},{4,5},{5,4},{6,7},{7,6},{8,9},{9,8},{10,11... | collective-permute-start | bytes 737288 | tf_op jit(solution)/shard_map/ppermute | solution.py:48
  23.8 19.7 %collective-permute-start.7 = (f32[64,1920]{1,0:T(8,128)S(1)}, f32[64,1920]{1,0:T(8,128)S(1)}, u32[]{:S(2)}, u32[]{:S(2)}) collective-permute-start(f32[64,1920]{1,0:T(8,128)S(1)} %get-tuple-element.108.refs_0_), channel_id=1, source_target_pairs={{0,16},{1,17},{2,18},{3,19},{4,20},{5,21},{6,22},{7,23},{8,24},{9,... | collective-permute-start | bytes 1474568 | tf_op jit(solution)/shard_map/ppermute | solution.py:48
  24.8 18.8 %collective-permute-start.8 = (f32[64,1920]{1,0:T(8,128)S(1)}, f32[64,1920]{1,0:T(8,128)S(1)}, u32[]{:S(2)}, u32[]{:S(2)}) collective-permute-start(f32[64,1920]{1,0:T(8,128)S(1)} %get-tuple-element.108.refs_0_), channel_id=1, source_target_pairs={{0,112},{1,113},{2,114},{3,115},{4,116},{5,117},{6,118},{7,119},{8... | collective-permute-start | bytes 1474568 | tf_op jit(solution)/shard_map/ppermute | solution.py:48
  31.3 7.7 %collective-permute-start.4 = (f32[2,8,1920]{2,1,0:T(8,128)S(1)}, f32[2,8,1920]{2,1,0:T(8,128)S(1)}, u32[]{:S(2)}, u32[]{:S(2)}) collective-permute-start(f32[2,8,1920]{2,1,0:T(8,128)S(1)} %get-tuple-element.79), channel_id=1, source_target_pairs={{0,6},{1,7},{2,0},{3,1},{4,2},{5,3},{6,4},{7,5},{8,14},{9,15},{10,... | collective-permute-start | bytes 368648 | tf_op jit(solution)/shard_map/ppermute | solution.py:48
  34.2 5.8 %collective-permute-start.5 = (f32[2,8,1920]{2,1,0:T(8,128)S(1)}, f32[2,8,1920]{2,1,0:T(8,128)S(1)}, u32[]{:S(2)}, u32[]{:S(2)}) collective-permute-start(f32[2,8,1920]{2,1,0:T(8,128)S(1)} %get-tuple-element.80), channel_id=1, source_target_pairs={{0,4},{1,5},{2,6},{3,7},{4,0},{5,1},{6,2},{7,3},{8,12},{9,13},{10,... | collective-permute-start | bytes 368648 | tf_op jit(solution)/shard_map/ppermute | solution.py:48
  34.5 9.0 %collective-permute-start.6 = (f32[2,8,1920]{2,1,0:T(8,128)S(1)}, f32[2,8,1920]{2,1,0:T(8,128)S(1)}, u32[]{:S(2)}, u32[]{:S(2)}) collective-permute-start(f32[2,8,1920]{2,1,0:T(8,128)S(1)} %get-tuple-element.81), channel_id=1, source_target_pairs={{0,2},{1,3},{2,4},{3,5},{4,6},{5,7},{6,0},{7,1},{8,10},{9,11},{10,... | collective-permute-start | bytes 368648 | tf_op jit(solution)/shard_map/ppermute | solution.py:48
  39.0 14.2 %collective-permute-start.11 = (f32[64,1920]{1,0:T(8,128)S(1)}, f32[64,1920]{1,0:T(8,128)S(1)}, u32[]{:S(2)}, u32[]{:S(2)}) collective-permute-start(f32[64,1920]{1,0:T(8,128)S(1)} %get-tuple-element.108.refs_0_), channel_id=1, source_target_pairs={{0,128},{1,129},{2,130},{3,131},{4,132},{5,133},{6,134},{7,135},{8... | collective-permute-start | bytes 1474568 | tf_op jit(solution)/shard_map/ppermute | solution.py:48
  43.5 13.5 %collective-permute-start.9 = (f32[64,1920]{1,0:T(8,128)S(1)}, f32[64,1920]{1,0:T(8,128)S(1)}, u32[]{:S(2)}, u32[]{:S(2)}) collective-permute-start(f32[64,1920]{1,0:T(8,128)S(1)} %collective-permute-done.7.refs_7_), channel_id=1, source_target_pairs={{0,16},{1,17},{2,18},{3,19},{4,20},{5,21},{6,22},{7,23},{8,24},{9,... | collective-permute-start | bytes 1474568 | tf_op jit(solution)/shard_map/ppermute | solution.py:48
  43.5 13.5 %collective-permute-start.10 = (f32[64,1920]{1,0:T(8,128)S(1)}, f32[64,1920]{1,0:T(8,128)S(1)}, u32[]{:S(2)}, u32[]{:S(2)}) collective-permute-start(f32[64,1920]{1,0:T(8,128)S(1)} %collective-permute-done.8.refs_1_), channel_id=1, source_target_pairs={{0,112},{1,113},{2,114},{3,115},{4,116},{5,117},{6,118},{7,119},{8... | collective-permute-start | bytes 1474568 | tf_op jit(solution)/shard_map/ppermute | solution.py:48
  47.8 19.0 %all-to-all-start = ((f32[16,2,8,480]{3,2,1,0:T(8,128)}), f32[16,2,8,480]{3,2,1,0:T(8,128)S(1)}, u32[]{:S(2)}, u32[]{:S(2)}) async-start(f32[16,2,8,480]{3,2,1,0:T(8,128)} %choose.1), calls=%async_computation | async-start | bytes 1048576 | tf_op jit(solution)/shard_map/all_to_all | solution.py:461
  53.2 16.6 %collective-permute-start.15 = (f32[64,1920]{1,0:T(8,128)S(1)}, f32[64,1920]{1,0:T(8,128)}, u32[]{:S(2)}, u32[]{:S(2)}) collective-permute-start(f32[64,1920]{1,0:T(8,128)S(1)} %collective-permute-done.8.refs_1_), channel_id=1, source_target_pairs={{0,128},{1,129},{2,130},{3,131},{4,132},{5,133},{6,134},{7,135},{8... | collective-permute-start | bytes 1474568 | tf_op jit(solution)/shard_map/ppermute | solution.py:48
  57.1 22.0 %collective-permute-start.13 = (f32[64,1920]{1,0:T(8,128)S(1)}, f32[64,1920]{1,0:T(8,128)}, u32[]{:S(2)}, u32[]{:S(2)}) collective-permute-start(f32[64,1920]{1,0:T(8,128)S(1)} %collective-permute-done.9.refs_6_), channel_id=1, source_target_pairs={{0,16},{1,17},{2,18},{3,19},{4,20},{5,21},{6,22},{7,23},{8,24},{9,... | collective-permute-start | bytes 1474568 | tf_op jit(solution)/shard_map/ppermute | solution.py:48
  57.1 22.0 %collective-permute-start.14 = (f32[64,1920]{1,0:T(8,128)S(1)}, f32[64,1920]{1,0:T(8,128)}, u32[]{:S(2)}, u32[]{:S(2)}) collective-permute-start(f32[64,1920]{1,0:T(8,128)S(1)} %collective-permute-done.10.refs_2_), channel_id=1, source_target_pairs={{0,112},{1,113},{2,114},{3,115},{4,116},{5,117},{6,118},{7,119},{8... | collective-permute-start | bytes 1474568 | tf_op jit(solution)/shard_map/ppermute | solution.py:48
  67.0 14.7 %collective-permute-start.12 = (f32[960,128]{1,0:T(8,128)S(1)}, f32[960,128]{1,0:T(8,128)S(1)}, u32[]{:S(2)}, u32[]{:S(2)}) collective-permute-start(f32[960,128]{1,0:T(8,128)S(1)} %turn.1.refs_0_), channel_id=1, source_target_pairs={{0,1},{1,0},{2,3},{3,2},{4,5},{5,4},{6,7},{7,6},{8,9},{9,8},{10,11... | collective-permute-start | bytes 1474568 | tf_op jit(solution)/shard_map/ppermute | solution.py:48
  68.9 12.8 %collective-permute-start.18 = (f32[960,128]{1,0:T(8,128)S(1)}, f32[960,128]{1,0:T(8,128)S(1)}, u32[]{:S(2)}, u32[]{:S(2)}) collective-permute-start(f32[960,128]{1,0:T(8,128)S(1)} %turn.1.refs_0_), channel_id=1, source_target_pairs={{0,2},{1,3},{2,4},{3,5},{4,6},{5,7},{6,0},{7,1},{8,10},{9,11},{10,... | collective-permute-start | bytes 1474568 | tf_op jit(solution)/shard_map/ppermute | solution.py:48
  69.8 14.6 %collective-permute-start.19 = (f32[960,128]{1,0:T(8,128)S(1)}, f32[960,128]{1,0:T(8,128)S(1)}, u32[]{:S(2)}, u32[]{:S(2)}) collective-permute-start(f32[960,128]{1,0:T(8,128)S(1)} %turn.1.refs_0_), channel_id=1, source_target_pairs={{0,6},{1,7},{2,0},{3,1},{4,2},{5,3},{6,4},{7,5},{8,14},{9,15},{10,... | collective-permute-start | bytes 1474568 | tf_op jit(solution)/shard_map/ppermute | solution.py:48
  79.0 12.7 %collective-permute-start.17 = (f32[64,1920]{1,0:T(8,128)S(1)}, f32[64,1920]{1,0:T(8,128)S(1)}, u32[]{:S(2)}, u32[]{:S(2)}) collective-permute-start(f32[64,1920]{1,0:T(8,128)S(1)} %collective-permute-done.11.refs_8_), channel_id=1, source_target_pairs={{0,16},{1,17},{2,18},{3,19},{4,20},{5,21},{6,22},{7,23},{8,24},{9,... | collective-permute-start | bytes 1474568 | tf_op jit(solution)/shard_map/ppermute | solution.py:48
  79.0 12.7 %collective-permute-start.20 = (f32[64,1920]{1,0:T(8,128)}, f32[64,1920]{1,0:T(8,128)S(1)}, u32[]{:S(2)}, u32[]{:S(2)}) collective-permute-start(f32[64,1920]{1,0:T(8,128)} %collective-permute-done.14.refs_0_), channel_id=1, source_target_pairs={{0,112},{1,113},{2,114},{3,115},{4,116},{5,117},{6,118},{7,119},{8... | collective-permute-start | bytes 1474568 | tf_op jit(solution)/shard_map/ppermute | solution.py:48
  81.7 14.1 %collective-permute-start.16 = (f32[960,128]{1,0:T(8,128)S(1)}, f32[960,128]{1,0:T(8,128)S(1)}, u32[]{:S(2)}, u32[]{:S(2)}) collective-permute-start(f32[960,128]{1,0:T(8,128)S(1)} %collective-permute-done.12.refs_1_), channel_id=1, source_target_pairs={{0,2},{1,3},{2,4},{3,5},{4,6},{5,7},{6,0},{7,1},{8,10},{9,11},{10,... | collective-permute-start | bytes 1474568 | tf_op jit(solution)/shard_map/ppermute | solution.py:48
  81.7 14.2 %collective-permute-start.22 = (f32[960,128]{1,0:T(8,128)S(1)}, f32[960,128]{1,0:T(8,128)S(1)}, u32[]{:S(2)}, u32[]{:S(2)}) collective-permute-start(f32[960,128]{1,0:T(8,128)S(1)} %collective-permute-done.12.refs_1_), channel_id=1, source_target_pairs={{0,6},{1,7},{2,0},{3,1},{4,2},{5,3},{6,4},{7,5},{8,14},{9,15},{10,... | collective-permute-start | bytes 1474568 | tf_op jit(solution)/shard_map/ppermute | solution.py:48
  84.4 11.5 %collective-permute-start.23 = (f32[64,1920]{1,0:T(8,128)}, f32[64,1920]{1,0:T(8,128)S(1)}, u32[]{:S(2)}, u32[]{:S(2)}) collective-permute-start(f32[64,1920]{1,0:T(8,128)} %collective-permute-done.14.refs_0_), channel_id=1, source_target_pairs={{0,128},{1,129},{2,130},{3,131},{4,132},{5,133},{6,134},{7,135},{8... | collective-permute-start | bytes 1474568 | tf_op jit(solution)/shard_map/ppermute | solution.py:48
  91.7 11.8 %collective-permute-start.26 = (f32[64,1920]{1,0:T(8,128)S(1)}, f32[64,1920]{1,0:T(8,128)S(1)}, u32[]{:S(2)}, u32[]{:S(2)}) collective-permute-start(f32[64,1920]{1,0:T(8,128)S(1)} %collective-permute-done.17.refs_11_.refs_15_), channel_id=1, source_target_pairs={{0,16},{1,17},{2,18},{3,19},{4,20},{5,21},{6,22},{7,23},{8,24},{9,... | collective-permute-start | bytes 1474568 | tf_op jit(solution)/shard_map/ppermute | solution.py:48
  92.5 11.0 %collective-permute-start.28 = (f32[64,1920]{1,0:T(8,128)}, f32[64,1920]{1,0:T(8,128)S(1)}, u32[]{:S(2)}, u32[]{:S(2)}) collective-permute-start(f32[64,1920]{1,0:T(8,128)} %collective-permute-done.15.refs_2_), channel_id=1, source_target_pairs={{0,112},{1,113},{2,114},{3,115},{4,116},{5,117},{6,118},{7,119},{8... | collective-permute-start | bytes 1474568 | tf_op jit(solution)/shard_map/ppermute | solution.py:48
  95.8 17.3 %collective-permute-start.25 = (f32[64,1920]{1,0:T(8,128)S(1)}, f32[64,1920]{1,0:T(8,128)S(1)}, u32[]{:S(2)}, u32[]{:S(2)}) collective-permute-start(f32[64,1920]{1,0:T(8,128)S(1)} %collective-permute-done.20.refs_4_), channel_id=1, source_target_pairs={{0,128},{1,129},{2,130},{3,131},{4,132},{5,133},{6,134},{7,135},{8... | collective-permute-start | bytes 1474568 | tf_op jit(solution)/shard_map/ppermute | solution.py:48
  95.9 17.2 %collective-permute-start.24 = (f32[960,128]{1,0:T(8,128)S(1)}, f32[960,128]{1,0:T(8,128)S(1)}, u32[]{:S(2)}, u32[]{:S(2)}) collective-permute-start(f32[960,128]{1,0:T(8,128)S(1)} %collective-permute-done.22.refs_3_), channel_id=1, source_target_pairs={{0,6},{1,7},{2,0},{3,1},{4,2},{5,3},{6,4},{7,5},{8,14},{9,15},{10,... | collective-permute-start | bytes 1474568 | tf_op jit(solution)/shard_map/ppermute | solution.py:48
  97.9 15.3 %collective-permute-start.21 = (f32[960,128]{1,0:T(8,128)S(1)}, f32[960,128]{1,0:T(8,128)S(1)}, u32[]{:S(2)}, u32[]{:S(2)}) collective-permute-start(f32[960,128]{1,0:T(8,128)S(1)} %collective-permute-done.18.refs_4_), channel_id=1, source_target_pairs={{0,2},{1,3},{2,4},{3,5},{4,6},{5,7},{6,0},{7,1},{8,10},{9,11},{10,... | collective-permute-start | bytes 1474568 | tf_op jit(solution)/shard_map/ppermute | solution.py:48
  103.5 10.8 %collective-permute-start.27 = (f32[64,1920]{1,0:T(8,128)S(1)}, f32[64,1920]{1,0:T(8,128)S(1)}, u32[]{:S(2)}, u32[]{:S(2)}) collective-permute-start(f32[64,1920]{1,0:T(8,128)S(1)} %collective-permute-done.26.refs_14_), channel_id=1, source_target_pairs={{0,16},{1,17},{2,18},{3,19},{4,20},{5,21},{6,22},{7,23},{8,24},{9,... | collective-permute-start | bytes 1474568 | tf_op jit(solution)/shard_map/ppermute | solution.py:48
  118.4 8.7 %collective-permute-start.30 = (f32[480,1280]{1,0:T(8,128)S(1)}, f32[480,1280]{1,0:T(8,128)S(1)}, u32[]{:S(2)}, u32[]{:S(2)}) collective-permute-start(f32[480,1280]{1,0:T(8,128)S(1)} %get-tuple-element.136), channel_id=1, source_target_pairs={{0,8},{1,9},{2,10},{3,11},{4,12},{5,13},{6,14},{7,15},{8,0},{9,1},... | collective-permute-start | bytes 7372808 | tf_op jit(solution)/shard_map/ppermute | solution.py:48
  125.3 3.5 %collective-permute-start.29 = (f32[480,640]{1,0:T(8,128)S(1)}, f32[480,640]{1,0:T(8,128)S(1)}, u32[]{:S(2)}, u32[]{:S(2)}) collective-permute-start(f32[480,640]{1,0:T(8,128)S(1)} %get-tuple-element.132), channel_id=1, source_target_pairs={{0,8},{1,9},{2,10},{3,11},{4,12},{5,13},{6,14},{7,15},{8,0},{9,1},... | collective-permute-start | bytes 3686408 | tf_op jit(solution)/shard_map/ppermute | solution.py:48
  (3 other events, 17.1 us)

commit v2 on v1

--- a/solution.py
+++ b/solution.py
@@ -17,7 +17,7 @@
 EVERY = 2048
 LAST = [(2, 0), (2, 1)]
 EARLY = [(dy, dxh) for dy in (0, 1, 3) for dxh in range(XH)]
-LATE = (NZ + 3, NZ + 4, NZ + 5, NZ + 6)
+LATE = (NZ + 4, NZ + 5)
 DEEP = 128 * len(LAST)
 PICK = SLOTS * len(LATE) * len(EARLY)
 MIB = 1 << 20
@@ -298,13 +298,14 @@
     lanes = slice(SLOTS * LATE[0], SLOTS * (LATE[-1] + 1))
     value = jnp.concatenate([shard[:, lanes] for shard in left], axis=1)
     high = value.astype(jnp.bfloat16).astype(jnp.float32)
-    out[...] = jnp.concatenate([high, value - high, high], axis=1).astype(jnp.bfloat16)
+    parts = [high, value - high, high, jnp.zeros_like(high)]
+    out[...] = jnp.concatenate(parts, axis=1).astype(jnp.bfloat16)
 
 
 def pick_late(left):
     return pl.pallas_call(
         pick_kernel,
-        out_shape=jax.ShapeDtypeStruct((CO * BLOCK, 3 * PICK), jnp.bfloat16),
+        out_shape=jax.ShapeDtypeStruct((CO * BLOCK, 4 * PICK), jnp.bfloat16),
         in_specs=[VMEM] * len(left),
         out_specs=VMEM,
         compiler_params=pltpu.CompilerParams(vmem_limit_bytes=12 * MIB),
@@ -336,7 +337,7 @@
 
 
 def early_kernel(lo, hi, left, *refs):
-    right, outs, stacked = refs[:12], refs[12:14], refs[14]
+    right, outs, stacked = refs[:14], refs[14:16], refs[16]
     depth = 128 * len(EARLY)
     none = jnp.zeros((SLOTS * len(LATE), hi - lo), jnp.float32)
     for j, place in enumerate(EARLY):
@@ -357,7 +358,7 @@
     return pl.pallas_call(
         functools.partial(early_kernel, lo, hi),
         out_shape=(out, out),
-        in_specs=[VMEM] * 13,
+        in_specs=[VMEM] * 15,
         out_specs=(VMEM, VMEM),
         scratch_shapes=[pltpu.VMEM((3 * depth, hi - lo), jnp.bfloat16)],
         compiler_params=pltpu.CompilerParams(vmem_limit_bytes=14 * MIB),
@@ -381,7 +382,7 @@
     across[:, 3 * DEEP :] = picked[...]
     pieces = [right[i][slot_rows(*place), lo:hi] for place in EARLY for i in LATE]
     high, low = split(jnp.concatenate(pieces, axis=0))
-    for part, value in enumerate((high, high, low)):
+    for part, value in enumerate((high, high, low, jnp.zeros_like(low))):
         stacked[3 * DEEP + PICK * part : 3 * DEEP + PICK * (part + 1), :] = value
     for i, out in enumerate(outs):
         out[...] = sums[i][...] + jnp.dot(
@@ -391,7 +392,7 @@
 
 def late_product(left, picked, right, lo, hi, sums):
     out = jax.ShapeDtypeStruct((BLOCK, hi - lo), jnp.float32)
-    depth = 3 * (DEEP + PICK)
+    depth = 3 * DEEP + 4 * PICK
     return pl.pallas_call(
         functools.partial(late_kernel, lo, hi),
         out_shape=(out, out),

time: 131 us -> 130 us (level)
  no operation moved by 1% of the time
where the time goes in v2:
time: 130 us; the launch traced here: 129 us
  starting transfers between devices  49 us (38%)
  waiting for transfers between devices  48 us (37%)
  Pallas kernels  29.6 us (23%)
  local copies, waits for them, and re-layouts  2.21 us (2%)
    ppermute x28, waiting for transfers between devices, send(): return lax.ppermute(value, AXES, pairs)  39.5 us
    ppermute x28, starting transfers between devices, send(): return lax.ppermute(value, AXES, pairs)  32.4 us
    ppermute x3, starting transfers between devices, shift_arc(): return lax.ppermute(value, AXES, pairs)  11.2 us
    pallas_call x2, Pallas kernels, early_product(): pl.pallas_call(functools.partial(early_kernel, lo, hi), out_shape=(out, o...  9.69 us
    all_to_all x1, waiting for transfers between devices, body(): lax.all_to_all(chosen, 'arc', 0, 0, axis_index_groups=same_core, tiled=True)  6.66 us
    pallas_call x2, Pallas kernels, late_product(): pl.pallas_call(functools.partial(late_kernel, lo, hi), out_shape=(out, ou...  5.53 us
    all_to_all x1, starting transfers between devices, body(): lax.all_to_all(chosen, 'arc', 0, 0, axis_index_groups=same_core, tiled=True)  5.46 us
    pallas_call x1, Pallas kernels, scan(): pl.pallas_call(scan_kernel, out_shape=(jax.ShapeDtypeStruct((8, WIDE + 12...  5.05 us
  transfers between devices with their start and end apart: 32, of which 14 were waited for; matrix products, arithmetic and copies ran while one was open for 0% of the time, Pallas kernels for 15%

profile of v2, /device:TPU:3, one launch (start us, length us, event | category | flops | bytes accessed | tf_op | source)
XLA Modules:
  0.0 129.2 jit_solution(12905731382817605548)
XLA Ops:
  0.0 5.0 %scan.1 = (f32[8,2048]{1,0:T(8,128)}, f32[64,256]{1,0:T(8,128)}, f32[3,64,1920]{2,1,0:T(8,128)}) custom-call(s32[32]{0:T(128)} %lengths_hbm.1, f32[6,6,64]{2,1,0:T(8,128)} %propagate_hbm.1, f32[6,64]{1,0:T(8,128)} %sight_hbm.1, f32[64]{0:T(128)} %weights_hbm.1, f32[3,64,1920]{2,1,0:T(8,128)} %force_hbm.1), custom_call_target="tpu_custom_call" | custom-call | tf_op jit(solution)/shard_map/scan/pallas_call | solution.py:126
  5.1 4.1 %collective-permute-start = (f32[8,2048]{1,0:T(8,128)}, f32[8,2048]{1,0:T(8,128)S(1)}, u32[]{:S(2)}, u32[]{:S(2)}) collective-permute-start(f32[8,2048]{1,0:T(8,128)} %get-tuple-element.69), channel_id=1, source_target_pairs={{0,8},{1,9},{2,10},{3,11},{4,12},{5,13},{6,14},{7,15},{8,16},{9,17... | collective-permute-start | bytes 196616 | tf_op jit(solution)/shard_map/ppermute | solution.py:442
  9.2 3.5 %collective-permute-start.1 = (f32[8,2048]{1,0:T(8,128)}, f32[8,2048]{1,0:T(8,128)S(1)}, u32[]{:S(2)}, u32[]{:S(2)}) collective-permute-start(f32[8,2048]{1,0:T(8,128)} %get-tuple-element.69), channel_id=1, source_target_pairs={{0,16},{1,17},{2,18},{3,19},{4,20},{5,21},{6,22},{7,23},{8,24},{9,... | collective-permute-start | bytes 196616 | tf_op jit(solution)/shard_map/ppermute | solution.py:442
  12.7 3.6 %collective-permute-start.2 = (f32[8,2048]{1,0:T(8,128)}, f32[8,2048]{1,0:T(8,128)S(1)}, u32[]{:S(2)}, u32[]{:S(2)}) collective-permute-start(f32[8,2048]{1,0:T(8,128)} %get-tuple-element.69), channel_id=1, source_target_pairs={{0,24},{1,25},{2,26},{3,27},{4,28},{5,29},{6,30},{7,31},{8,32},{9,... | collective-permute-start | bytes 196616 | tf_op jit(solution)/shard_map/ppermute | solution.py:442
  19.5 1.8 %collective-permute-done.2.three = f32[8,2048]{1,0:T(8,128)S(1)} collective-permute-done((f32[8,2048]{1,0:T(8,128)}, f32[8,2048]{1,0:T(8,128)S(1)}, u32[]{:S(2)}, u32[]{:S(2)}) %collective-permute-start.2) | collective-permute-done | bytes 65568 | tf_op jit(solution)/shard_map/ppermute | solution.py:442
  21.8 2.0 %collective-permute-start.3 = (f32[4,8,1920]{2,1,0:T(8,128)S(1)}, f32[4,8,1920]{2,1,0:T(8,128)S(1)}, u32[]{:S(2)}, u32[]{:S(2)}) collective-permute-start(f32[4,8,1920]{2,1,0:T(8,128)S(1)} %get-tuple-element.73), channel_id=1, source_target_pairs={{0,1},{1,0},{2,3},{3,2},{4,5},{5,4},{6,7},{7,6},{8,9},{9,8},{10,11... | collective-permute-start | bytes 737288 | tf_op jit(solution)/shard_map/ppermute | solution.py:48
  24.8 1.8 %collective-permute-start.8 = (f32[64,1920]{1,0:T(8,128)S(1)}, f32[64,1920]{1,0:T(8,128)S(1)}, u32[]{:S(2)}, u32[]{:S(2)}) collective-permute-start(f32[64,1920]{1,0:T(8,128)S(1)} %get-tuple-element.105.refs_0_), channel_id=1, source_target_pairs={{0,112},{1,113},{2,114},{3,115},{4,116},{5,117},{6,118},{7,119},{8... | collective-permute-start | bytes 1474568 | tf_op jit(solution)/shard_map/ppermute | solution.py:48
  26.5 4.8 %collective-permute-done.3.second = f32[4,8,1920]{2,1,0:T(8,128)S(1)} collective-permute-done((f32[4,8,1920]{2,1,0:T(8,128)S(1)}, f32[4,8,1920]{2,1,0:T(8,128)S(1)}, u32[]{:S(2)}, u32[]{:S(2)}) %collective-permute-start.3) | collective-permute-done | bytes 245792 | tf_op jit(solution)/shard_map/ppermute | solution.py:48
  31.3 2.8 %collective-permute-start.4 = (f32[2,8,1920]{2,1,0:T(8,128)S(1)}, f32[2,8,1920]{2,1,0:T(8,128)S(1)}, u32[]{:S(2)}, u32[]{:S(2)}) collective-permute-start(f32[2,8,1920]{2,1,0:T(8,128)S(1)} %get-tuple-element.77), channel_id=1, source_target_pairs={{0,6},{1,7},{2,0},{3,1},{4,2},{5,3},{6,4},{7,5},{8,14},{9,15},{10,... | collective-permute-start | bytes 368648 | tf_op jit(solution)/shard_map/ppermute | solution.py:48
  35.2 3.8 %collective-permute-done.4.refs_1_ = f32[2,8,1920]{2,1,0:T(8,128)S(1)} collective-permute-done((f32[2,8,1920]{2,1,0:T(8,128)S(1)}, f32[2,8,1920]{2,1,0:T(8,128)S(1)}, u32[]{:S(2)}, u32[]{:S(2)}) %collective-permute-start.4) | collective-permute-done | bytes 122912 | tf_op jit(solution)/shard_map/ppermute | solution.py:48
  39.9 3.6 %collective-permute-done.6.refs_3_ = f32[2,8,1920]{2,1,0:T(8,128)S(1)} collective-permute-done((f32[2,8,1920]{2,1,0:T(8,128)S(1)}, f32[2,8,1920]{2,1,0:T(8,128)S(1)}, u32[]{:S(2)}, u32[]{:S(2)}) %collective-permute-start.6) | collective-permute-done | bytes 122912 | tf_op jit(solution)/shard_map/ppermute | solution.py:48
  43.5 2.7 %collective-permute-start.10 = (f32[64,1920]{1,0:T(8,128)S(1)}, f32[64,1920]{1,0:T(8,128)S(1)}, u32[]{:S(2)}, u32[]{:S(2)}) collective-permute-start(f32[64,1920]{1,0:T(8,128)S(1)} %collective-permute-done.8.refs_1_), channel_id=1, source_target_pairs={{0,112},{1,113},{2,114},{3,115},{4,116},{5,117},{6,118},{7,119},{8... | collective-permute-start | bytes 1474568 | tf_op jit(solution)/shard_map/ppermute | solution.py:48
  46.2 1.6 %choose.1 = f32[16,2,8,480]{3,2,1,0:T(8,128)} custom-call(s32[32]{0:T(128)S(1)} %copy-done.2, f32[2,8,1920]{2,1,0:T(8,128)S(1)} %get-tuple-element.80.refs_0_, f32[2,8,1920]{2,1,0:T(8,128)S(1)} %collective-permute-done.4.refs_1_, f32[2,8,1920]{2,1,0:T(8,128)S(1)} %collective-permute-done.5.refs_2_, f32[2,8,1920]{2,1,0:T(8,128)S(1)} %collective-permute-done.6.refs_3_), custom_call_target="tpu_custom_call" | custom-call | tf_op jit(solution)/shard_map/choose/pallas_call | solution.py:237
  47.8 5.5 %all-to-all-start = ((f32[16,2,8,480]{3,2,1,0:T(8,128)}), f32[16,2,8,480]{3,2,1,0:T(8,128)S(1)}, u32[]{:S(2)}, u32[]{:S(2)}) async-start(f32[16,2,8,480]{3,2,1,0:T(8,128)} %choose.1), calls=%async_computation | async-start | bytes 1048576 | tf_op jit(solution)/shard_map/all_to_all | solution.py:462
  53.4 3.6 %collective-permute-done.9.refs_6_ = f32[64,1920]{1,0:T(8,128)S(1)} collective-permute-done((f32[64,1920]{1,0:T(8,128)S(1)}, f32[64,1920]{1,0:T(8,128)S(1)}, u32[]{:S(2)}, u32[]{:S(2)}) %collective-permute-start.9) | collective-permute-done | bytes 491552 | tf_op jit(solution)/shard_map/ppermute | solution.py:48
  57.1 3.0 %collective-permute-start.14 = (f32[64,1920]{1,0:T(8,128)S(1)}, f32[64,1920]{1,0:T(8,128)}, u32[]{:S(2)}, u32[]{:S(2)}) collective-permute-start(f32[64,1920]{1,0:T(8,128)S(1)} %collective-permute-done.10.refs_2_), channel_id=1, source_target_pairs={{0,112},{1,113},{2,114},{3,115},{4,116},{5,117},{6,118},{7,119},{8... | collective-permute-start | bytes 1474568 | tf_op jit(solution)/shard_map/ppermute | solution.py:48
  60.1 6.7 %all-to-all-done.pieces = f32[16,2,8,480]{3,2,1,0:T(8,128)S(1)} async-done(((f32[16,2,8,480]{3,2,1,0:T(8,128)}), f32[16,2,8,480]{3,2,1,0:T(8,128)S(1)}, u32[]{:S(2)}, u32[]{:S(2)}) %all-to-all-start) | async-done | bytes 491552 | tf_op jit(solution)/shard_map/all_to_all | solution.py:462
  67.0 1.9 %collective-permute-start.12 = (f32[960,128]{1,0:T(8,128)S(1)}, f32[960,128]{1,0:T(8,128)S(1)}, u32[]{:S(2)}, u32[]{:S(2)}) collective-permute-start(f32[960,128]{1,0:T(8,128)S(1)} %turn.1.refs_0_), channel_id=1, source_target_pairs={{0,1},{1,0},{2,3},{3,2},{4,5},{5,4},{6,7},{7,6},{8,9},{9,8},{10,11... | collective-permute-start | bytes 1474568 | tf_op jit(solution)/shard_map/ppermute | solution.py:48
  69.8 1.7 %collective-permute-start.19 = (f32[960,128]{1,0:T(8,128)S(1)}, f32[960,128]{1,0:T(8,128)S(1)}, u32[]{:S(2)}, u32[]{:S(2)}) collective-permute-start(f32[960,128]{1,0:T(8,128)S(1)} %turn.1.refs_0_), channel_id=1, source_target_pairs={{0,6},{1,7},{2,0},{3,1},{4,2},{5,3},{6,4},{7,5},{8,14},{9,15},{10,... | collective-permute-start | bytes 1474568 | tf_op jit(solution)/shard_map/ppermute | solution.py:48
  71.6 7.5 %collective-permute-done.13.refs_1_ = f32[64,1920]{1,0:T(8,128)} collective-permute-done((f32[64,1920]{1,0:T(8,128)S(1)}, f32[64,1920]{1,0:T(8,128)}, u32[]{:S(2)}, u32[]{:S(2)}) %collective-permute-start.13) | collective-permute-done | bytes 491552 | tf_op jit(solution)/shard_map/ppermute | solution.py:48
  79.0 2.7 %collective-permute-start.20 = (f32[64,1920]{1,0:T(8,128)}, f32[64,1920]{1,0:T(8,128)S(1)}, u32[]{:S(2)}, u32[]{:S(2)}) collective-permute-start(f32[64,1920]{1,0:T(8,128)} %collective-permute-done.14.refs_0_), channel_id=1, source_target_pairs={{0,112},{1,113},{2,114},{3,115},{4,116},{5,117},{6,118},{7,119},{8... | collective-permute-start | bytes 1474568 | tf_op jit(solution)/shard_map/ppermute | solution.py:48
  81.7 2.7 %collective-permute-start.22 = (f32[960,128]{1,0:T(8,128)S(1)}, f32[960,128]{1,0:T(8,128)S(1)}, u32[]{:S(2)}, u32[]{:S(2)}) collective-permute-start(f32[960,128]{1,0:T(8,128)S(1)} %collective-permute-done.12.refs_1_), channel_id=1, source_target_pairs={{0,6},{1,7},{2,0},{3,1},{4,2},{5,3},{6,4},{7,5},{8,14},{9,15},{10,... | collective-permute-start | bytes 1474568 | tf_op jit(solution)/shard_map/ppermute | solution.py:48
  84.7 7.0 %collective-permute-done.17.refs_13_.refs_15_ = f32[64,1920]{1,0:T(8,128)S(1)} collective-permute-done((f32[64,1920]{1,0:T(8,128)S(1)}, f32[64,1920]{1,0:T(8,128)S(1)}, u32[]{:S(2)}, u32[]{:S(2)}) %collective-permute-start.17) | collective-permute-done | bytes 491552 | tf_op jit(solution)/shard_map/ppermute | solution.py:48
  92.5 1.9 %collective-permute-start.28 = (f32[64,1920]{1,0:T(8,128)}, f32[64,1920]{1,0:T(8,128)S(1)}, u32[]{:S(2)}, u32[]{:S(2)}) collective-permute-start(f32[64,1920]{1,0:T(8,128)} %collective-permute-done.15.refs_2_), channel_id=1, source_target_pairs={{0,112},{1,113},{2,114},{3,115},{4,116},{5,117},{6,118},{7,119},{8... | collective-permute-start | bytes 1474568 | tf_op jit(solution)/shard_map/ppermute | solution.py:48
  99.4 4.1 %collective-permute-done.26.refs_12_.refs_14_ = f32[64,1920]{1,0:T(8,128)S(1)} collective-permute-done((f32[64,1920]{1,0:T(8,128)S(1)}, f32[64,1920]{1,0:T(8,128)S(1)}, u32[]{:S(2)}, u32[]{:S(2)}) %collective-permute-start.26) | collective-permute-done | bytes 491552 | tf_op jit(solution)/shard_map/ppermute | solution.py:48
  103.5 3.7 %early.3 = (f32[480,640]{1,0:T(8,128)S(1)}, f32[480,640]{1,0:T(8,128)S(1)}) custom-call(bf16[960,2304]{1,0:T(8,128)(2,1)S(1)} %stack.1.left, f32[64,1920]{1,0:T(8,128)S(1)} %get-tuple-element.105.refs_0_, f32[64,1920]{1,0:T(8,128)S(1)} %collective-permute-done.8.refs_1_, f32[64,1920]{1,0:T(8,128)S(1)} %collective-permute-done.10.refs_2_, ...), custom_call_target="tpu_custom_call" | custom-call | flops 2831155200 | bytes 14000000 | tf_op jit(solution)/shard_map/early/pallas_call | solution.py:358
  107.2 6.0 %early.2 = (f32[480,1280]{1,0:T(8,128)S(1)}, f32[480,1280]{1,0:T(8,128)S(1)}) custom-call(bf16[960,2304]{1,0:T(8,128)(2,1)S(1)} %stack.1.left, f32[64,1920]{1,0:T(8,128)S(1)} %get-tuple-element.105.refs_0_, f32[64,1920]{1,0:T(8,128)S(1)} %collective-permute-done.8.refs_1_, f32[64,1920]{1,0:T(8,128)S(1)} %collective-permute-done.10.refs_2_, ...), custom_call_target="tpu_custom_call" | custom-call | flops 5662310400 | bytes 14000000 | tf_op jit(solution)/shard_map/early/pallas_call | solution.py:358
  114.3 3.4 %late.3 = (f32[480,1280]{1,0:T(8,128)S(1)}, f32[480,1280]{1,0:T(8,128)S(1)}) custom-call(f32[960,128]{1,0:T(8,128)S(1)} %collective-permute-done.21.first, f32[960,128]{1,0:T(8,128)S(1)} %collective-permute-done.24.second, bf16[960,384]{1,0:T(8,128)(2,1)S(1)} %pick.1.picked, f32[64,1920]{1,0:T(8,128)S(1)} %get-tuple-element.105.refs_0_, ...), custom_call_target="tpu_custom_call" | custom-call | flops 2831155200 | bytes 14000000 | tf_op jit(solution)/shard_map/late/pallas_call | solution.py:396
  117.7 4.1 %collective-permute-start.30 = (f32[480,1280]{1,0:T(8,128)S(1)}, f32[480,1280]{1,0:T(8,128)S(1)}, u32[]{:S(2)}, u32[]{:S(2)}) collective-permute-start(f32[480,1280]{1,0:T(8,128)S(1)} %get-tuple-element.132), channel_id=1, source_target_pairs={{0,8},{1,9},{2,10},{3,11},{4,12},{5,13},{6,14},{7,15},{8,0},{9,1},... | collective-permute-start | bytes 7372808 | tf_op jit(solution)/shard_map/ppermute | solution.py:48
  121.8 2.1 %late.2 = (f32[480,640]{1,0:T(8,128)S(1)}, f32[480,640]{1,0:T(8,128)S(1)}) custom-call(f32[960,128]{1,0:T(8,128)S(1)} %collective-permute-done.21.first, f32[960,128]{1,0:T(8,128)S(1)} %collective-permute-done.24.second, bf16[960,384]{1,0:T(8,128)(2,1)S(1)} %pick.1.picked, f32[64,1920]{1,0:T(8,128)S(1)} %get-tuple-element.105.refs_0_, ...), custom_call_target="tpu_custom_call" | custom-call | flops 1415577600 | bytes 14000000 | tf_op jit(solution)/shard_map/late/pallas_call | solution.py:396
  124.0 2.1 %collective-permute-done.30.passed = f32[480,1280]{1,0:T(8,128)S(1)} collective-permute-done((f32[480,1280]{1,0:T(8,128)S(1)}, f32[480,1280]{1,0:T(8,128)S(1)}, u32[]{:S(2)}, u32[]{:S(2)}) %collective-permute-start.30) | collective-permute-done | bytes 2457632 | tf_op jit(solution)/shard_map/ppermute | solution.py:48
  126.1 1.7 %finish.2.refs_0_ = f32[480,1920]{1,0:T(8,128)} custom-call(f32[480,1280]{1,0:T(8,128)S(1)} %get-tuple-element.131.mine, f32[480,1280]{1,0:T(8,128)S(1)} %collective-permute-done.30.passed), custom_call_target="tpu_custom_call" | custom-call | tf_op jit(solution)/shard_map/finish/pallas_call | solution.py:423
  (53 shorter events, 16.4 us)
Async XLA Ops:
  5.1 14.5 %collective-permute-start = (f32[8,2048]{1,0:T(8,128)}, f32[8,2048]{1,0:T(8,128)S(1)}, u32[]{:S(2)}, u32[]{:S(2)}) collective-permute-start(f32[8,2048]{1,0:T(8,128)} %get-tuple-element.69), channel_id=1, source_target_pairs={{0,8},{1,9},{2,10},{3,11},{4,12},{5,13},{6,14},{7,15},{8,16},{9,17... | collective-permute-start | bytes 196616 | tf_op jit(solution)/shard_map/ppermute | solution.py:442
  9.2 10.4 %collective-permute-start.1 = (f32[8,2048]{1,0:T(8,128)}, f32[8,2048]{1,0:T(8,128)S(1)}, u32[]{:S(2)}, u32[]{:S(2)}) collective-permute-start(f32[8,2048]{1,0:T(8,128)} %get-tuple-element.69), channel_id=1, source_target_pairs={{0,16},{1,17},{2,18},{3,19},{4,20},{5,21},{6,22},{7,23},{8,24},{9,... | collective-permute-start | bytes 196616 | tf_op jit(solution)/shard_map/ppermute | solution.py:442
  12.7 8.6 %collective-permute-start.2 = (f32[8,2048]{1,0:T(8,128)}, f32[8,2048]{1,0:T(8,128)S(1)}, u32[]{:S(2)}, u32[]{:S(2)}) collective-permute-start(f32[8,2048]{1,0:T(8,128)} %get-tuple-element.69), channel_id=1, source_target_pairs={{0,24},{1,25},{2,26},{3,27},{4,28},{5,29},{6,30},{7,31},{8,32},{9,... | collective-permute-start | bytes 196616 | tf_op jit(solution)/shard_map/ppermute | solution.py:442
  21.8 9.5 %collective-permute-start.3 = (f32[4,8,1920]{2,1,0:T(8,128)S(1)}, f32[4,8,1920]{2,1,0:T(8,128)S(1)}, u32[]{:S(2)}, u32[]{:S(2)}) collective-permute-start(f32[4,8,1920]{2,1,0:T(8,128)S(1)} %get-tuple-element.73), channel_id=1, source_target_pairs={{0,1},{1,0},{2,3},{3,2},{4,5},{5,4},{6,7},{7,6},{8,9},{9,8},{10,11... | collective-permute-start | bytes 737288 | tf_op jit(solution)/shard_map/ppermute | solution.py:48
  23.8 19.7 %collective-permute-start.7 = (f32[64,1920]{1,0:T(8,128)S(1)}, f32[64,1920]{1,0:T(8,128)S(1)}, u32[]{:S(2)}, u32[]{:S(2)}) collective-permute-start(f32[64,1920]{1,0:T(8,128)S(1)} %get-tuple-element.105.refs_0_), channel_id=1, source_target_pairs={{0,16},{1,17},{2,18},{3,19},{4,20},{5,21},{6,22},{7,23},{8,24},{9,... | collective-permute-start | bytes 1474568 | tf_op jit(solution)/shard_map/ppermute | solution.py:48
  24.8 18.8 %collective-permute-start.8 = (f32[64,1920]{1,0:T(8,128)S(1)}, f32[64,1920]{1,0:T(8,128)S(1)}, u32[]{:S(2)}, u32[]{:S(2)}) collective-permute-start(f32[64,1920]{1,0:T(8,128)S(1)} %get-tuple-element.105.refs_0_), channel_id=1, source_target_pairs={{0,112},{1,113},{2,114},{3,115},{4,116},{5,117},{6,118},{7,119},{8... | collective-permute-start | bytes 1474568 | tf_op jit(solution)/shard_map/ppermute | solution.py:48
  31.3 7.7 %collective-permute-start.4 = (f32[2,8,1920]{2,1,0:T(8,128)S(1)}, f32[2,8,1920]{2,1,0:T(8,128)S(1)}, u32[]{:S(2)}, u32[]{:S(2)}) collective-permute-start(f32[2,8,1920]{2,1,0:T(8,128)S(1)} %get-tuple-element.77), channel_id=1, source_target_pairs={{0,6},{1,7},{2,0},{3,1},{4,2},{5,3},{6,4},{7,5},{8,14},{9,15},{10,... | collective-permute-start | bytes 368648 | tf_op jit(solution)/shard_map/ppermute | solution.py:48
  34.2 5.8 %collective-permute-start.5 = (f32[2,8,1920]{2,1,0:T(8,128)S(1)}, f32[2,8,1920]{2,1,0:T(8,128)S(1)}, u32[]{:S(2)}, u32[]{:S(2)}) collective-permute-start(f32[2,8,1920]{2,1,0:T(8,128)S(1)} %get-tuple-element.78), channel_id=1, source_target_pairs={{0,4},{1,5},{2,6},{3,7},{4,0},{5,1},{6,2},{7,3},{8,12},{9,13},{10,... | collective-permute-start | bytes 368648 | tf_op jit(solution)/shard_map/ppermute | solution.py:48
  34.5 9.0 %collective-permute-start.6 = (f32[2,8,1920]{2,1,0:T(8,128)S(1)}, f32[2,8,1920]{2,1,0:T(8,128)S(1)}, u32[]{:S(2)}, u32[]{:S(2)}) collective-permute-start(f32[2,8,1920]{2,1,0:T(8,128)S(1)} %get-tuple-element.79), channel_id=1, source_target_pairs={{0,2},{1,3},{2,4},{3,5},{4,6},{5,7},{6,0},{7,1},{8,10},{9,11},{10,... | collective-permute-start | bytes 368648 | tf_op jit(solution)/shard_map/ppermute | solution.py:48
  39.0 14.2 %collective-permute-start.11 = (f32[64,1920]{1,0:T(8,128)S(1)}, f32[64,1920]{1,0:T(8,128)S(1)}, u32[]{:S(2)}, u32[]{:S(2)}) collective-permute-start(f32[64,1920]{1,0:T(8,128)S(1)} %get-tuple-element.105.refs_0_), channel_id=1, source_target_pairs={{0,128},{1,129},{2,130},{3,131},{4,132},{5,133},{6,134},{7,135},{8... | collective-permute-start | bytes 1474568 | tf_op jit(solution)/shard_map/ppermute | solution.py:48
  43.5 13.5 %collective-permute-start.9 = (f32[64,1920]{1,0:T(8,128)S(1)}, f32[64,1920]{1,0:T(8,128)S(1)}, u32[]{:S(2)}, u32[]{:S(2)}) collective-permute-start(f32[64,1920]{1,0:T(8,128)S(1)} %collective-permute-done.7.refs_7_), channel_id=1, source_target_pairs={{0,16},{1,17},{2,18},{3,19},{4,20},{5,21},{6,22},{7,23},{8,24},{9,... | collective-permute-start | bytes 1474568 | tf_op jit(solution)/shard_map/ppermute | solution.py:48
  43.5 13.5 %collective-permute-start.10 = (f32[64,1920]{1,0:T(8,128)S(1)}, f32[64,1920]{1,0:T(8,128)S(1)}, u32[]{:S(2)}, u32[]{:S(2)}) collective-permute-start(f32[64,1920]{1,0:T(8,128)S(1)} %collective-permute-done.8.refs_1_), channel_id=1, source_target_pairs={{0,112},{1,113},{2,114},{3,115},{4,116},{5,117},{6,118},{7,119},{8... | collective-permute-start | bytes 1474568 | tf_op jit(solution)/shard_map/ppermute | solution.py:48
  47.8 19.0 %all-to-all-start = ((f32[16,2,8,480]{3,2,1,0:T(8,128)}), f32[16,2,8,480]{3,2,1,0:T(8,128)S(1)}, u32[]{:S(2)}, u32[]{:S(2)}) async-start(f32[16,2,8,480]{3,2,1,0:T(8,128)} %choose.1), calls=%async_computation | async-start | bytes 1048576 | tf_op jit(solution)/shard_map/all_to_all | solution.py:462
  53.2 16.6 %collective-permute-start.15 = (f32[64,1920]{1,0:T(8,128)S(1)}, f32[64,1920]{1,0:T(8,128)}, u32[]{:S(2)}, u32[]{:S(2)}) collective-permute-start(f32[64,1920]{1,0:T(8,128)S(1)} %collective-permute-done.8.refs_1_), channel_id=1, source_target_pairs={{0,128},{1,129},{2,130},{3,131},{4,132},{5,133},{6,134},{7,135},{8... | collective-permute-start | bytes 1474568 | tf_op jit(solution)/shard_map/ppermute | solution.py:48
  57.1 22.0 %collective-permute-start.13 = (f32[64,1920]{1,0:T(8,128)S(1)}, f32[64,1920]{1,0:T(8,128)}, u32[]{:S(2)}, u32[]{:S(2)}) collective-permute-start(f32[64,1920]{1,0:T(8,128)S(1)} %collective-permute-done.9.refs_6_), channel_id=1, source_target_pairs={{0,16},{1,17},{2,18},{3,19},{4,20},{5,21},{6,22},{7,23},{8,24},{9,... | collective-permute-start | bytes 1474568 | tf_op jit(solution)/shard_map/ppermute | solution.py:48
  57.1 22.0 %collective-permute-start.14 = (f32[64,1920]{1,0:T(8,128)S(1)}, f32[64,1920]{1,0:T(8,128)}, u32[]{:S(2)}, u32[]{:S(2)}) collective-permute-start(f32[64,1920]{1,0:T(8,128)S(1)} %collective-permute-done.10.refs_2_), channel_id=1, source_target_pairs={{0,112},{1,113},{2,114},{3,115},{4,116},{5,117},{6,118},{7,119},{8... | collective-permute-start | bytes 1474568 | tf_op jit(solution)/shard_map/ppermute | solution.py:48
  67.0 14.7 %collective-permute-start.12 = (f32[960,128]{1,0:T(8,128)S(1)}, f32[960,128]{1,0:T(8,128)S(1)}, u32[]{:S(2)}, u32[]{:S(2)}) collective-permute-start(f32[960,128]{1,0:T(8,128)S(1)} %turn.1.refs_0_), channel_id=1, source_target_pairs={{0,1},{1,0},{2,3},{3,2},{4,5},{5,4},{6,7},{7,6},{8,9},{9,8},{10,11... | collective-permute-start | bytes 1474568 | tf_op jit(solution)/shard_map/ppermute | solution.py:48
  68.9 12.8 %collective-permute-start.18 = (f32[960,128]{1,0:T(8,128)S(1)}, f32[960,128]{1,0:T(8,128)S(1)}, u32[]{:S(2)}, u32[]{:S(2)}) collective-permute-start(f32[960,128]{1,0:T(8,128)S(1)} %turn.1.refs_0_), channel_id=1, source_target_pairs={{0,2},{1,3},{2,4},{3,5},{4,6},{5,7},{6,0},{7,1},{8,10},{9,11},{10,... | collective-permute-start | bytes 1474568 | tf_op jit(solution)/shard_map/ppermute | solution.py:48
  69.8 14.6 %collective-permute-start.19 = (f32[960,128]{1,0:T(8,128)S(1)}, f32[960,128]{1,0:T(8,128)S(1)}, u32[]{:S(2)}, u32[]{:S(2)}) collective-permute-start(f32[960,128]{1,0:T(8,128)S(1)} %turn.1.refs_0_), channel_id=1, source_target_pairs={{0,6},{1,7},{2,0},{3,1},{4,2},{5,3},{6,4},{7,5},{8,14},{9,15},{10,... | collective-permute-start | bytes 1474568 | tf_op jit(solution)/shard_map/ppermute | solution.py:48
  79.0 12.7 %collective-permute-start.17 = (f32[64,1920]{1,0:T(8,128)S(1)}, f32[64,1920]{1,0:T(8,128)S(1)}, u32[]{:S(2)}, u32[]{:S(2)}) collective-permute-start(f32[64,1920]{1,0:T(8,128)S(1)} %collective-permute-done.11.refs_8_), channel_id=1, source_target_pairs={{0,16},{1,17},{2,18},{3,19},{4,20},{5,21},{6,22},{7,23},{8,24},{9,... | collective-permute-start | bytes 1474568 | tf_op jit(solution)/shard_map/ppermute | solution.py:48
  79.0 12.7 %collective-permute-start.20 = (f32[64,1920]{1,0:T(8,128)}, f32[64,1920]{1,0:T(8,128)S(1)}, u32[]{:S(2)}, u32[]{:S(2)}) collective-permute-start(f32[64,1920]{1,0:T(8,128)} %collective-permute-done.14.refs_0_), channel_id=1, source_target_pairs={{0,112},{1,113},{2,114},{3,115},{4,116},{5,117},{6,118},{7,119},{8... | collective-permute-start | bytes 1474568 | tf_op jit(solution)/shard_map/ppermute | solution.py:48
  81.7 14.1 %collective-permute-start.16 = (f32[960,128]{1,0:T(8,128)S(1)}, f32[960,128]{1,0:T(8,128)S(1)}, u32[]{:S(2)}, u32[]{:S(2)}) collective-permute-start(f32[960,128]{1,0:T(8,128)S(1)} %collective-permute-done.12.refs_1_), channel_id=1, source_target_pairs={{0,2},{1,3},{2,4},{3,5},{4,6},{5,7},{6,0},{7,1},{8,10},{9,11},{10,... | collective-permute-start | bytes 1474568 | tf_op jit(solution)/shard_map/ppermute | solution.py:48
  81.7 14.2 %collective-permute-start.22 = (f32[960,128]{1,0:T(8,128)S(1)}, f32[960,128]{1,0:T(8,128)S(1)}, u32[]{:S(2)}, u32[]{:S(2)}) collective-permute-start(f32[960,128]{1,0:T(8,128)S(1)} %collective-permute-done.12.refs_1_), channel_id=1, source_target_pairs={{0,6},{1,7},{2,0},{3,1},{4,2},{5,3},{6,4},{7,5},{8,14},{9,15},{10,... | collective-permute-start | bytes 1474568 | tf_op jit(solution)/shard_map/ppermute | solution.py:48
  84.4 11.5 %collective-permute-start.23 = (f32[64,1920]{1,0:T(8,128)}, f32[64,1920]{1,0:T(8,128)S(1)}, u32[]{:S(2)}, u32[]{:S(2)}) collective-permute-start(f32[64,1920]{1,0:T(8,128)} %collective-permute-done.14.refs_0_), channel_id=1, source_target_pairs={{0,128},{1,129},{2,130},{3,131},{4,132},{5,133},{6,134},{7,135},{8... | collective-permute-start | bytes 1474568 | tf_op jit(solution)/shard_map/ppermute | solution.py:48
  91.7 11.8 %collective-permute-start.26 = (f32[64,1920]{1,0:T(8,128)S(1)}, f32[64,1920]{1,0:T(8,128)S(1)}, u32[]{:S(2)}, u32[]{:S(2)}) collective-permute-start(f32[64,1920]{1,0:T(8,128)S(1)} %collective-permute-done.17.refs_13_.refs_15_), channel_id=1, source_target_pairs={{0,16},{1,17},{2,18},{3,19},{4,20},{5,21},{6,22},{7,23},{8,24},{9,... | collective-permute-start | bytes 1474568 | tf_op jit(solution)/shard_map/ppermute | solution.py:48
  92.5 11.0 %collective-permute-start.28 = (f32[64,1920]{1,0:T(8,128)}, f32[64,1920]{1,0:T(8,128)S(1)}, u32[]{:S(2)}, u32[]{:S(2)}) collective-permute-start(f32[64,1920]{1,0:T(8,128)} %collective-permute-done.15.refs_2_), channel_id=1, source_target_pairs={{0,112},{1,113},{2,114},{3,115},{4,116},{5,117},{6,118},{7,119},{8... | collective-permute-start | bytes 1474568 | tf_op jit(solution)/shard_map/ppermute | solution.py:48
  95.8 17.4 %collective-permute-start.25 = (f32[64,1920]{1,0:T(8,128)S(1)}, f32[64,1920]{1,0:T(8,128)S(1)}, u32[]{:S(2)}, u32[]{:S(2)}) collective-permute-start(f32[64,1920]{1,0:T(8,128)S(1)} %collective-permute-done.20.refs_4_), channel_id=1, source_target_pairs={{0,128},{1,129},{2,130},{3,131},{4,132},{5,133},{6,134},{7,135},{8... | collective-permute-start | bytes 1474568 | tf_op jit(solution)/shard_map/ppermute | solution.py:48
  95.9 17.3 %collective-permute-start.24 = (f32[960,128]{1,0:T(8,128)S(1)}, f32[960,128]{1,0:T(8,128)S(1)}, u32[]{:S(2)}, u32[]{:S(2)}) collective-permute-start(f32[960,128]{1,0:T(8,128)S(1)} %collective-permute-done.22.refs_3_), channel_id=1, source_target_pairs={{0,6},{1,7},{2,0},{3,1},{4,2},{5,3},{6,4},{7,5},{8,14},{9,15},{10,... | collective-permute-start | bytes 1474568 | tf_op jit(solution)/shard_map/ppermute | solution.py:48
  97.9 15.2 %collective-permute-start.21 = (f32[960,128]{1,0:T(8,128)S(1)}, f32[960,128]{1,0:T(8,128)S(1)}, u32[]{:S(2)}, u32[]{:S(2)}) collective-permute-start(f32[960,128]{1,0:T(8,128)S(1)} %collective-permute-done.18.refs_4_), channel_id=1, source_target_pairs={{0,2},{1,3},{2,4},{3,5},{4,6},{5,7},{6,0},{7,1},{8,10},{9,11},{10,... | collective-permute-start | bytes 1474568 | tf_op jit(solution)/shard_map/ppermute | solution.py:48
  103.5 10.8 %collective-permute-start.27 = (f32[64,1920]{1,0:T(8,128)S(1)}, f32[64,1920]{1,0:T(8,128)S(1)}, u32[]{:S(2)}, u32[]{:S(2)}) collective-permute-start(f32[64,1920]{1,0:T(8,128)S(1)} %collective-permute-done.26.refs_12_.refs_14_), channel_id=1, source_target_pairs={{0,16},{1,17},{2,18},{3,19},{4,20},{5,21},{6,22},{7,23},{8,24},{9,... | collective-permute-start | bytes 1474568 | tf_op jit(solution)/shard_map/ppermute | solution.py:48
  117.7 8.4 %collective-permute-start.30 = (f32[480,1280]{1,0:T(8,128)S(1)}, f32[480,1280]{1,0:T(8,128)S(1)}, u32[]{:S(2)}, u32[]{:S(2)}) collective-permute-start(f32[480,1280]{1,0:T(8,128)S(1)} %get-tuple-element.132), channel_id=1, source_target_pairs={{0,8},{1,9},{2,10},{3,11},{4,12},{5,13},{6,14},{7,15},{8,0},{9,1},... | collective-permute-start | bytes 7372808 | tf_op jit(solution)/shard_map/ppermute | solution.py:48
  123.9 3.9 %collective-permute-start.29 = (f32[480,640]{1,0:T(8,128)S(1)}, f32[480,640]{1,0:T(8,128)S(1)}, u32[]{:S(2)}, u32[]{:S(2)}) collective-permute-start(f32[480,640]{1,0:T(8,128)S(1)} %get-tuple-element.128), channel_id=1, source_target_pairs={{0,8},{1,9},{2,10},{3,11},{4,12},{5,13},{6,14},{7,15},{8,0},{9,1},... | collective-permute-start | bytes 3686408 | tf_op jit(solution)/shard_map/ppermute | solution.py:48
  (3 other events, 17.1 us)
